TPU v7x, 32 devices: a whole 2x2x4 slice. The times are simulated.
32 devices in a mesh: seq: 8 (over y, x, core), fsdp: 4 (over z).
Axes of the slice: x: 2, y: 2, z: 4, core: 2. Of those that a mesh axis runs over, the one named last changes fastest.
Arguments:
- queries: bfloat16 [2048, 3072], P('seq', 'fsdp'), may hold values from -64 to 64
- key_rows: bfloat16 [2048, 3072], P('seq', 'fsdp'), may hold values from -4 to 4
- value_rows: bfloat16 [2048, 3072], P('seq', 'fsdp'), may hold values from -6 to 6
- pattern: int32 [16, 8], P('seq'), may hold values from 0 to 15, as said below
- out_weight: bfloat16 [128, 24, 6144], P('seq', None, 'fsdp'), may hold values from -0.109375 to 0.109375
- out_grad: bfloat16 [2048, 6144], P('seq', 'fsdp'), may hold values from -6 to 6
Outputs:
- projected: bfloat16 [2048, 6144], P('seq', 'fsdp')
- query_grad: bfloat16 [2048, 3072], P('seq', 'fsdp')
- key_grad: bfloat16 [2048, 3072], P('seq', 'fsdp')
- value_grad: bfloat16 [2048, 3072], P('seq', 'fsdp')
- weight_grad: float32 [128, 24, 6144], P('seq', None, 'fsdp')
Inputs may be any that keep to these rules, and one draw needn't show every extreme that they name: `pattern`: row i holds (i - 1) mod 16, i and (i + 1) mod 16 in columns 0 to 2; columns 3 and 4 hold the same two different blocks in every row; in columns 5 to 7, the 2 rows from any multiple of 2 name blocks of any one range o * 2 to (o + 1) * 2 - 1 at most 1 times together, and some range exactly 1 times.
All inputs are finite; a program needn't handle non-finite values.
Results may differ from a plain program's by a relative error of at most 0.035.
Values may be sent and summed in bfloat16 or wider, within the bound.
A program may use at most 128 MiB of HBM per device.

v0:
```python
import math

import jax
import jax.numpy as jnp
from jax import lax
from jax.sharding import PartitionSpec as P

HD = 128
BLK = 128
NWIN = 3
NGLOB = 2
NRAND = 3
NSEL = 8


def padded_2(cells, sides, width):
    for axis, dim in sides:
        count = lax.axis_size(axis)
        head = lax.slice_in_dim(cells, 0, width, axis=dim)
        tail = lax.slice_in_dim(cells, cells.shape[dim] - width, cells.shape[dim], axis=dim)
        cells = jnp.concatenate(
            [
                lax.ppermute(tail, axis, [(i, (i + 1) % count) for i in range(count)]),
                cells,
                lax.ppermute(head, axis, [((i + 1) % count, i) for i in range(count)]),
            ],
            axis=dim,
        )
    return cells


def broadcast(value, axis, root):
    mine = lax.axis_index(axis) == root
    return lax.psum(jnp.where(mine, value, jnp.zeros_like(value)), axis)


def shards(queries, key_rows, value_rows, pattern, out_weight, out_grad):
    row_count, width_here = queries.shape
    blocks = row_count // BLK
    heads_here = width_here // HD
    seq_count = lax.axis_size("seq")
    seq_index = lax.axis_index("seq")
    score_scale = 1.0 / math.sqrt(HD)
    slots_each = (NRAND * blocks + seq_count - 1) // seq_count
    slot_total = seq_count * slots_each
    kv_blocks = jnp.stack(
        [key_rows.reshape(blocks, BLK, width_here), value_rows.reshape(blocks, BLK, width_here)],
        axis=1,
    )
    padded = padded_2(kv_blocks, (("seq", 0),), 1)
    window = jnp.stack([padded[0:blocks], padded[1 : blocks + 1], padded[2 : blocks + 2]], axis=1)
    global_ids = pattern[0, NWIN : NWIN + NGLOB]
    global_list = []
    for global_pos in range(NGLOB):
        global_id = global_ids[global_pos]
        own_block = lax.dynamic_index_in_dim(kv_blocks, global_id % blocks, 0, keepdims=False)
        global_list.append(broadcast(own_block, "seq", global_id // blocks))
    global_kv = jnp.stack(global_list, axis=0)
    wanted_ids = pattern[:, NWIN + NGLOB :].reshape(-1)
    req_total = wanted_ids.shape[0]
    owner_of = wanted_ids // blocks
    positions = jnp.arange(req_total, dtype=jnp.int32)
    same_owner = (owner_of[:, None] == owner_of[None, :]).astype(jnp.int32)
    earlier = (positions[None, :] < positions[:, None]).astype(jnp.int32)
    slot_of = owner_of * slots_each + jnp.sum(same_owner * earlier, axis=1)
    slot_ids = jnp.arange(slot_total, dtype=jnp.int32)
    matches = (slot_of[:, None] == slot_ids[None, :]).astype(jnp.int32)
    slot_used = jnp.sum(matches, axis=0)
    slot_request = jnp.sum(matches * positions[:, None], axis=0)
    send_ids = jnp.sum(matches * (wanted_ids[:, None] + 1), axis=0) - 1
    asked = lax.all_to_all(
        send_ids.reshape(seq_count, slots_each), "seq", split_axis=0, concat_axis=0, tiled=True
    ).reshape(slot_total)
    asked_local = asked - seq_index * blocks
    asked_valid = asked >= 0
    picked = jnp.take(kv_blocks, jnp.clip(asked_local, 0, blocks - 1), axis=0)
    picked = jnp.where(asked_valid[:, None, None, None], picked, jnp.zeros_like(picked))
    arrived = lax.all_to_all(
        picked.reshape(seq_count, slots_each, 2, BLK, width_here),
        "seq",
        split_axis=0,
        concat_axis=0,
        tiled=True,
    )
    random_kv = jnp.take(arrived.reshape(slot_total, 2, BLK, width_here), slot_of, axis=0).reshape(
        blocks, NRAND, 2, BLK, width_here
    )
    global_rep = jnp.broadcast_to(global_kv[None], (blocks, NGLOB, 2, BLK, width_here))
    all_kv = jnp.concatenate([window, global_rep, random_kv], axis=1)
    key_set = all_kv[:, :, 0].reshape(blocks, NSEL * BLK, heads_here, HD)
    value_set = all_kv[:, :, 1].reshape(blocks, NSEL * BLK, heads_here, HD)
    query_four = queries.reshape(blocks, BLK, heads_here, HD)
    scores = (
        jnp.einsum("jqhd,jkhd->jhqk", query_four, key_set, preferred_element_type=jnp.float32)
        * score_scale
    )
    probs = jax.nn.softmax(scores, axis=-1)
    probs_low = probs.astype(jnp.bfloat16)
    attended = jnp.einsum(
        "jhqk,jkhd->jqhd", probs_low, value_set, preferred_element_type=jnp.float32
    ).astype(jnp.bfloat16)
    attended = attended.reshape(row_count, width_here)
    attended_all = lax.all_gather(attended, "fsdp", axis=1, tiled=True)
    attended_three = attended_all.reshape(row_count, attended_all.shape[1] // HD, HD)
    full_weight = lax.all_gather(out_weight, "seq", axis=0, tiled=True)
    proj_sum = jnp.einsum(
        "the,ehc->tc", attended_three, full_weight, preferred_element_type=jnp.float32
    )
    head_part = jnp.einsum("tc,ehc->the", out_grad, full_weight, preferred_element_type=jnp.float32)
    projected = proj_sum.astype(jnp.bfloat16)
    rounded_part = lax.optimization_barrier(head_part.astype(jnp.bfloat16)).astype(jnp.float32)
    head_grad = lax.psum_scatter(
        rounded_part.astype(jnp.bfloat16), "fsdp", scatter_dimension=1, tiled=True
    )
    local_grad = jnp.einsum(
        "the,tc->ehc", attended_three, out_grad, preferred_element_type=jnp.float32
    )
    rounded_grad = lax.optimization_barrier(local_grad.astype(jnp.bfloat16)).astype(jnp.float32)
    weight_grad = lax.psum_scatter(
        rounded_grad.astype(jnp.bfloat16), "seq", scatter_dimension=0, tiled=True
    ).astype(jnp.float32)
    grad_four = head_grad.reshape(blocks, BLK, heads_here, HD)
    prob_grad = jnp.einsum(
        "jqhd,jkhd->jhqk", grad_four, value_set, preferred_element_type=jnp.float32
    )
    center = jnp.sum(probs * prob_grad, axis=-1, keepdims=True)
    score_grad = (probs * (prob_grad - center)).astype(jnp.bfloat16)
    query_grad = (
        jnp.einsum("jhqk,jkhd->jqhd", score_grad, key_set, preferred_element_type=jnp.float32)
        * score_scale
    ).astype(jnp.bfloat16)
    query_grad = query_grad.reshape(row_count, width_here)
    key_terms = (
        jnp.einsum("jhqk,jqhd->jkhd", score_grad, query_four, preferred_element_type=jnp.float32)
        * score_scale
    ).astype(jnp.bfloat16)
    value_terms = jnp.einsum(
        "jhqk,jqhd->jkhd", probs_low, grad_four, preferred_element_type=jnp.float32
    ).astype(jnp.bfloat16)
    slot_terms = jnp.stack(
        [
            key_terms.reshape(blocks, NSEL, BLK, width_here),
            value_terms.reshape(blocks, NSEL, BLK, width_here),
        ],
        axis=2,
    )
    window_terms = slot_terms[:, :NWIN].astype(jnp.float32)
    acc_padded = jnp.zeros((blocks + 2, 2, BLK, width_here), jnp.float32)
    for offset in range(NWIN):
        acc_padded = acc_padded + jnp.pad(
            window_terms[:, offset], ((offset, NWIN - 1 - offset), (0, 0), (0, 0), (0, 0))
        )
    edges = jnp.stack([acc_padded[0], acc_padded[blocks + 1]], axis=0).astype(jnp.bfloat16)
    from_beside = padded_2(edges, (("seq", 0),), 1)
    own_acc = acc_padded[1 : blocks + 1]
    own_acc = own_acc.at[0].add(from_beside[0].astype(jnp.float32))
    own_acc = own_acc.at[blocks - 1].add(from_beside[3].astype(jnp.float32))
    global_terms = jnp.sum(slot_terms[:, NWIN : NWIN + NGLOB].astype(jnp.float32), axis=0)
    global_total = lax.psum(global_terms.astype(jnp.bfloat16), "seq").astype(jnp.float32)
    block_iota = jnp.arange(blocks, dtype=jnp.int32)
    global_mask = (global_ids // blocks == seq_index)[:, None] & (
        (global_ids % blocks)[:, None] == block_iota[None, :]
    )
    own_acc = own_acc + jnp.sum(
        global_mask.astype(jnp.float32)[:, :, None, None, None] * global_total[:, None], axis=0
    )
    random_terms = slot_terms[:, NWIN + NGLOB :].reshape(req_total, 2, BLK, width_here)
    send_back = jnp.take(random_terms, slot_request, axis=0)
    send_back = jnp.where(
        (slot_used > 0)[:, None, None, None], send_back, jnp.zeros_like(send_back)
    )
    returned = lax.all_to_all(
        send_back.reshape(seq_count, slots_each, 2, BLK, width_here),
        "seq",
        split_axis=0,
        concat_axis=0,
        tiled=True,
    )
    returned = returned.reshape(slot_total, 2 * BLK * width_here)
    owner_table = ((asked_local[:, None] == block_iota[None, :]) & asked_valid[:, None]).astype(
        jnp.bfloat16
    )
    random_sum = jnp.einsum("sq,sx->qx", owner_table, returned, preferred_element_type=jnp.float32)
    own_acc = own_acc + random_sum.reshape(blocks, 2, BLK, width_here)
    key_grad = own_acc[:, 0].astype(jnp.bfloat16).reshape(row_count, width_here)
    value_grad = own_acc[:, 1].astype(jnp.bfloat16).reshape(row_count, width_here)
    return (projected, query_grad, key_grad, value_grad, weight_grad)


def solution(mesh):
    placed = (
        P("seq", "fsdp"),
        P("seq", "fsdp"),
        P("seq", "fsdp"),
        P("seq", None),
        P("seq", None, "fsdp"),
        P("seq", "fsdp"),
    )
    return jax.shard_map(
        shards,
        mesh=mesh,
        in_specs=placed,
        out_specs=(
            P("seq", "fsdp"),
            P("seq", "fsdp"),
            P("seq", "fsdp"),
            P("seq", "fsdp"),
            P("seq", None, "fsdp"),
        ),
        check_vma=False,
    )
```

profile of v0, /device:TPU:9, one launch (start us, length us, event | category | flops | bytes accessed | tf_op | source)
XLA Modules:
  0.0 403.0 jit_solution(1927811288629942358)
XLA Ops:
  7.2 1.4 fusion.75
  13.9 2.7 fusion.41
  16.7 1.4 copy.211
  20.3 4.4 %all-to-all-start = ((s32[8,1,1]{2,1,0:T(1,128)}), s32[8,1,1]{2,1,0:T(1,128)S(1)}, u32[]{:S(2)}, u32[]{:S(2)}) async-start(s32[8,1,1]{2,1,0:T(1,128)} %copy.199), calls=%async_computation | async-start | bytes 8192 | tf_op jit(solution)/shard_map/all_to_all | solution.py:71
  24.8 3.8 all-to-all-done
  29.0 2.4 gather_fusion
  31.7 4.0 fusion.10
  35.7 5.2 %all-to-all-start.1 = ((bf16[8,1,2,128,768]{4,3,2,1,0:T(8,128)(2,1)}), bf16[8,1,2,128,768]{4,3,2,1,0:T(8,128)(2,1)}, u32[]{:S(2)}, u32[]{:S(2)}) async-start(bf16[8,1,2,128,768]{4,3,2,1,0:T(8,128)(2,1)} %fusion.10), calls=%async_computation.1 | async-start | bytes 6291456 | tf_op jit(solution)/shard_map/all_to_all | solution.py:78
  40.9 1.7 collective-permute-start
  43.2 1.2 fusion.66
  44.9 1.2 reduce_sum.82
  46.2 1.2 reshape.512
  48.1 1.3 compare_and_fusion.2
  49.4 38.5 %collective-permute-done = bf16[1,2,128,768]{3,2,1,0:T(8,128)(2,1)S(1)} collective-permute-done((bf16[1,2,128,768]{3,2,1,0:T(8,128)(2,1)S(1)}, bf16[1,2,128,768]{3,2,1,0:T(8,128)(2,1)S(1)}, u32[]{:S(2)}, u32[]{:S(2)}) %collective-permute-start) | collective-permute-done | bytes 393248 | tf_op jit(solution)/shard_map/ppermute | solution.py:23
  87.9 0.9 fusion.35
  88.8 0.9 bitcast_dynamic-update-slice_fusion
  89.8 1.2 pad_maximum_fusion.6
  91.0 0.9 fusion.33
  91.9 1.3 broadcast_dynamic-update-slice_fusion
  93.2 2.9 gather_fusion.1
  96.1 2.0 select_dynamic-update-slice_fusion
  98.2 6.2 %fusion.72 = (bf16[2,8,1,128,768]{4,3,2,1,0:T(8,128)(2,1)}, bf16[2,8,1,128,768]{4,3,2,1,0:T(8,128)(2,1)}) fusion(bf16[2,8,2,128,768]{4,3,2,1,0:T(8,128)(2,1)} %select_dynamic-update-slice_fusion), kind=kLoop, calls=%fused_computation.153 | loop fusion | bytes 12582912 | tf_op jit(solution)/shard_map/slice | solution.py:90
  104.3 5.0 %copy.205 = bf16[2,8,1,128,768]{3,1,4,0,2:T(8,128)(2,1)} copy(bf16[2,8,1,128,768]{4,3,2,1,0:T(8,128)(2,1)} %get-tuple-element.77) | data formatting | bytes 6291456 | tf_op jit(solution)/shard_map/slice | solution.py:90
  109.3 5.8 %reshape_squeeze.7 = bf16[2,1024,6,128]{1,3,2,0:T(8,128)(2,1)} reshape(bf16[2,8,1,128,768]{3,1,4,0,2:T(8,128)(2,1)} %copy.205) | data formatting | bytes 6291456 | tf_op jit(solution)/shard_map/reshape;squeeze | solution.py:90
  115.1 5.2 %copy.204 = bf16[2,8,1,128,768]{3,1,4,0,2:T(8,128)(2,1)} copy(bf16[2,8,1,128,768]{4,3,2,1,0:T(8,128)(2,1)} %get-tuple-element.78) | data formatting | bytes 6291456 | tf_op jit(solution)/shard_map/slice | solution.py:91
  120.3 5.9 %reshape_squeeze.6 = bf16[2,1024,6,128]{1,3,2,0:T(8,128)(2,1)} reshape(bf16[2,8,1,128,768]{3,1,4,0,2:T(8,128)(2,1)} %copy.204) | data formatting | bytes 6291456 | tf_op jit(solution)/shard_map/reshape;squeeze | solution.py:91
  126.2 7.0 %fusion.76 = (f32[2,6,128]{2,1,0:T(8,128)S(1)}, f32[2,6,128,1024]{2,3,1,0:T(8,128)}) fusion(bf16[2,1024,6,128]{1,3,2,0:T(8,128)(2,1)} %reshape_squeeze.7, bf16[2,128,6,128]{3,2,1,0:T(8,128)(2,1)S(1)} %copy-done.9), kind=kOutput, calls=%fused_computation.157 | convolution fusion | flops 407372800 | bytes 9836544 | tf_op jit(solution)/shard_map/sub | solution.py:97
  133.2 4.8 %fusion.26 = bf16[2,128,6,128]{1,3,2,0:T(8,128)(2,1)S(1)} fusion(bf16[2,1024,6,128]{1,3,2,0:T(8,128)(2,1)} %reshape_squeeze.6, f32[2,6,128,1024]{2,3,1,0:T(8,128)} %get-tuple-element.95, f32[2,6,128]{2,1,0:T(8,128)S(1)} %get-tuple-element.94), kind=kOutput, calls=%fused_computation.50 | convolution fusion | flops 405995520 | bytes 9836544 | tf_op jit(solution)/shard_map/jhqk,jkhd->jqhd/dot_general | solution.py:99
  139.4 5.2 %all-gather.5.cloned.1.call-done = bf16[128,24,1536]{2,0,1:T(8,128)(2,1)} async-done(((bf16[16,24,1536]{2,0,1:T(8,128)(2,1)}), bf16[128,24,1536]{2,0,1:T(8,128)(2,1)}) %all-gather.5.cloned.1.call-update) | async-done | bytes 9437200 | tf_op jit(solution)/shard_map/all_gather | solution.py:105
  144.7 7.5 %fusion.21 = bf16[256,24,128]{0,2,1:T(8,128)(2,1)} fusion(bf16[128,24,1536]{2,0,1:T(8,128)(2,1)} %all-gather.5.cloned.1.call-done, bf16[256,1536]{1,0:T(8,128)(2,1)S(1)} %copy-done), kind=kOutput, calls=%fused_computation.46 | convolution fusion | flops 2416705536 | bytes 11796480 | tf_op jit(solution)/shard_map/tc,ehc->the/dot_general | solution.py:109
  152.2 30.1 %all-gather.3.cloned.1.call-done = bf16[256,3072]{0,1:T(8,128)(2,1)} async-done(((bf16[256,768]{0,1:T(8,128)(2,1)}), bf16[256,3072]{0,1:T(8,128)(2,1)}) %all-gather.3.cloned.1.call-update) | async-done | bytes 1572880 | tf_op jit(solution)/shard_map/all_gather | solution.py:103
  182.3 6.6 %convert_bitcast_fusion = bf16[128,24,1536]{2,0,1:T(8,128)(2,1)} fusion(bf16[256,24,128]{0,2,1:T(8,128)(2,1)} %bitcast.186, bf16[256,1536]{1,0:T(8,128)(2,1)S(1)} %copy-done), kind=kOutput, calls=%fused_computation.4 | convolution fusion | flops 2420637696 | bytes 11796480 | tf_op jit(solution)/shard_map/the,tc->ehc/dot_general | solution.py:115
  189.6 28.9 %reduce-scatter.3.cloned.1.call-done = bf16[256,6,128]{0,2,1:T(8,128)(2,1)} async-done(((bf16[256,24,128]{0,2,1:T(8,128)(2,1)}), bf16[256,6,128]{0,2,1:T(8,128)(2,1)}) %reduce-scatter.3.cloned.1.call-update) | async-done | bytes 393232 | tf_op jit(solution)/shard_map/reduce_scatter | solution.py:112
  218.5 3.9 convolution_convert_fusion
  222.5 2.5 copy.246
  225.0 3.8 copy.224
  228.8 6.6 %multiply_reduce_fusion = (f32[2,6,128]{2,1,0:T(8,128)S(1)}, f32[2,6,128,1024]{2,3,1,0:T(8,128)S(1)}) fusion(f32[2,6,128,1024]{2,3,1,0:T(8,128)} %get-tuple-element.95, f32[2,6,128]{2,1,0:T(8,128)S(1)} %get-tuple-element.94, bf16[2,1024,6,128]{1,3,2,0:T(8,128)(2,1)} %reshape_squeeze.6, bf16[256,6,128]{0,2,1:T(8,128)(2,1)} %reduce-scatter.3.cloned.1.call-done), kind=kOutput, calls=%fused_computation.15 | convolution fusion | flops 407370240 | bytes 16134144 | tf_op jit(solution)/shard_map/jqhd,jkhd->jhqk/dot_general | solution.py:123
  235.4 5.0 %multiply_convert_fusion.1 = bf16[2,6,128,1024]{2,3,1,0:T(8,128)(2,1)S(1)} fusion(f32[2,6,128,1024]{2,3,1,0:T(8,128)S(1)} %get-tuple-element.97, f32[2,6,128]{2,1,0:T(8,128)S(1)} %get-tuple-element.96, f32[2,6,128,1024]{2,3,1,0:T(8,128)} %get-tuple-element.95, f32[2,6,128]{2,1,0:T(8,128)S(1)} %get-tuple-element.94), kind=kLoop, calls=%fused_computation.14 | loop fusion | flops 6291456 | bytes 15740928 | tf_op jit(solution)/shard_map/convert_element_type | solution.py:127
  240.4 1.7 copy-done.3
  242.2 2.6 fusion.6
  244.8 4.6 %copy.220 = bf16[2,1024,6,128]{1,3,2,0:T(8,128)(2,1)} copy(bf16[2,1024,6,128]{3,1,2,0:T(8,128)(2,1)} %fusion.6) | data formatting | bytes 6291456 | tf_op jit(solution)/shard_map/convert_element_type | solution.py:136
  249.4 4.5 %copy.245 = bf16[192,8,8,128]{3,2,1,0:T(8,128)(2,1)} copy(bf16[192,8,8,128]{3,1,2,0:T(8,128)(2,1)} %bitcast.184) | data formatting | bytes 6291456
  253.9 5.0 %copy.223 = bf16[2,8,1,128,768]{4,3,2,0,1:T(8,128)(2,1)} copy(bf16[2,8,1,128,768]{3,1,4,0,2:T(8,128)(2,1)} %bitcast.185) | data formatting | bytes 6291456 | tf_op jit(solution)/shard_map/stack;reshape | solution.py:140
  258.9 3.7 fusion.14
  262.6 1.6 copy.225
  264.2 4.4 %gather_fusion.2 = bf16[8,2,128,768]{3,2,1,0:T(8,128)(2,1)} fusion(bf16[6,2,128,768]{3,2,1,0:T(8,128)(2,1)} %bitcast.181, s32[1024]{0:T(1024)S(1)} %get-tuple-element.100), kind=kCustom, calls=%fused_computation.2 | custom fusion | bytes 6291488 | tf_op jit(solution)/shard_map/jit(_take)/gather | solution.py:168
  268.6 4.0 %fusion.8 = bf16[8,1,2,128,768]{4,3,2,1,0:T(8,128)(2,1)} fusion(bf16[8,2,128,768]{3,2,1,0:T(8,128)(2,1)} %gather_fusion.2, pred[8]{0:T(512)(128)(4,1)S(1)} %get-tuple-element.98, pred[8]{0:T(512)(128)(4,1)S(1)} %get-tuple-element.99), kind=kLoop, calls=%fused_computation.20 | loop fusion | flops 3145728 | bytes 6291472 | tf_op jit(solution)/shard_map/jit(_where)/select_n | solution.py:169
  272.6 6.4 %all-to-all-start.2 = ((bf16[8,1,2,128,768]{4,3,2,1,0:T(8,128)(2,1)}), bf16[8,1,2,128,768]{4,3,2,1,0:T(8,128)(2,1)}, u32[]{:S(2)}, u32[]{:S(2)}) async-start(bf16[8,1,2,128,768]{4,3,2,1,0:T(8,128)(2,1)} %fusion.8), calls=%async_computation.3 | async-start | bytes 6291456 | tf_op jit(solution)/shard_map/all_to_all | solution.py:172
  279.1 7.7 %fusion.12 = bf16[256,1536]{1,0:T(8,128)(2,1)} fusion(bf16[256,24,128]{0,2,1:T(8,128)(2,1)} %bitcast.187, bf16[128,24,1536]{2,0,1:T(8,128)(2,1)} %all-gather.5.cloned.1.call-done), kind=kOutput, calls=%fused_computation.29 | convolution fusion | flops 2416312320 | bytes 11796480 | tf_op jit(solution)/shard_map/the,ehc->tc/dot_general | solution.py:106
  286.7 33.8 %reduce-scatter.5.cloned.1.call-done = bf16[16,24,1536]{2,0,1:T(8,128)(2,1)} async-done(((bf16[128,24,1536]{2,0,1:T(8,128)(2,1)}), bf16[16,24,1536]{2,0,1:T(8,128)(2,1)}) %reduce-scatter.5.cloned.1.call-update) | async-done | bytes 1179664 | tf_op jit(solution)/shard_map/reduce_scatter | solution.py:119
  320.5 3.5 copy.229
  324.1 1.4 fusion.16
  325.5 2.9 slice_bitcast_fusion.2
  328.4 2.1 fusion.71
  330.6 6.7 %collective-permute-start.2 = (bf16[1,2,128,768]{3,2,1,0:T(8,128)(2,1)S(1)}, bf16[1,2,128,768]{3,2,1,0:T(8,128)(2,1)S(1)}, u32[]{:S(2)}, u32[]{:S(2)}) collective-permute-start(bf16[1,2,128,768]{3,2,1,0:T(8,128)(2,1)S(1)} %get-tuple-element.83), channel_id=1, source_target_pairs={{0,4},{4,8},{8,12},{12,16},{16,20},{20,24},{24,28},{28,0},{1,5},{5... | collective-permute-start | bytes 1179656 | tf_op jit(solution)/shard_map/ppermute | solution.py:23
  337.3 1.0 fusion.29
  339.4 1.5 slice.170
  340.9 44.7 %all-reduce.7.cloned.1.call-done = bf16[2,2,128,768]{3,2,1,0:T(8,128)(2,1)} async-done(((bf16[2,2,128,768]{3,2,1,0:T(8,128)(2,1)}), bf16[2,2,128,768]{3,2,1,0:T(8,128)(2,1)}) %all-reduce.7.cloned.1.call-update) | async-done | bytes 786448 | tf_op jit(solution)/shard_map/psum | solution.py:159
  385.6 1.3 convert_element_type.118
  386.9 1.5 multiply_reduce_fusion.1
  388.4 1.2 fusion.31
  389.8 3.6 copy.247
  393.5 1.0 fusion.59
  395.2 0.9 fusion.74
  (97 shorter events, 9.3 us)
Async XLA Ops:
  7.2 137.5 %copy-start = (bf16[256,1536]{1,0:T(8,128)(2,1)S(1)}, bf16[256,1536]{1,0:T(8,128)(2,1)}, u32[]{:S(2)}) copy-start(bf16[256,1536]{1,0:T(8,128)(2,1)} %param.15) | copy-start | bytes 2359300
  7.2 9.5 %copy-start.11 = (bf16[16,24,1536]{2,1,0:T(8,128)(2,1)S(1)}, bf16[16,24,1536]{2,1,0:T(8,128)(2,1)}, u32[]{:S(2)}) copy-start(bf16[16,24,1536]{2,1,0:T(8,128)(2,1)} %param.14) | copy-start | bytes 3538948
  7.2 82.6 %all-reduce.9.cloned.1.call-start = ((), (), s32[]{:S(2)}) async-start(), calls=%async_computation.10 | async-start | bytes 1572864 | tf_op jit(solution)/shard_map/psum | solution.py:34
  13.9 4.2 %copy-start.15 = (s32[2,8]{1,0:T(2,128)S(1)}, s32[2,8]{1,0:T(2,128)}, u32[]{:S(2)}) copy-start(s32[2,8]{1,0:T(2,128)} %param.13) | copy-start | bytes 196
  13.9 10.8 %copy-start.6 = (bf16[256,768]{1,0:T(8,128)(2,1)S(1)}, bf16[256,768]{1,0:T(8,128)(2,1)}, u32[]{:S(2)}) copy-start(bf16[256,768]{1,0:T(8,128)(2,1)} %param.11) | copy-start | bytes 1179652
  13.9 10.8 %copy-start.7 = (bf16[256,768]{1,0:T(8,128)(2,1)S(1)}, bf16[256,768]{1,0:T(8,128)(2,1)}, u32[]{:S(2)}) copy-start(bf16[256,768]{1,0:T(8,128)(2,1)} %param.12) | copy-start | bytes 1179652
  16.7 128.0 %all-gather.5.cloned.1.call-start = ((), (), s32[]{:S(2)}) async-start(), calls=%async_computation.6 | async-start | bytes 10616832 | tf_op jit(solution)/shard_map/all_gather | solution.py:105
  18.2 6.5 %copy-start.22 = (s32[2,3]{1,0:T(2,128)}, s32[2,3]{1,0:T(2,128)S(1)}, u32[]{:S(2)}) copy-start(s32[2,3]{1,0:T(2,128)S(1)} %slice.136) | copy-start | bytes 76
  18.5 0.5 copy-start.24
  19.6 24.8 %copy-start.20 = (s32[8]{0:T(128)}, s32[8]{0:T(128)S(1)}, u32[]{:S(2)}) copy-start(s32[8]{0:T(128)S(1)} %get-tuple-element.67) | copy-start | bytes 100
  20.3 8.3 %all-to-all-start = ((s32[8,1,1]{2,1,0:T(1,128)}), s32[8,1,1]{2,1,0:T(1,128)S(1)}, u32[]{:S(2)}, u32[]{:S(2)}) async-start(s32[8,1,1]{2,1,0:T(1,128)} %copy.199), calls=%async_computation | async-start | bytes 8192 | tf_op jit(solution)/shard_map/all_to_all | solution.py:71
  29.0 2.7 copy-start.17
  35.7 5.2 %copy-start.14 = (bf16[1,2,128,768]{3,2,1,0:T(8,128)(2,1)S(1)}, bf16[1,2,128,768]{3,2,1,0:T(8,128)(2,1)}, u32[]{:S(2)}) copy-start(bf16[1,2,128,768]{3,2,1,0:T(8,128)(2,1)} %get-tuple-element.87) | copy-start | bytes 1179652
  35.7 6.9 %copy-start.13 = (bf16[1,2,128,768]{3,2,1,0:T(8,128)(2,1)S(1)}, bf16[1,2,128,768]{3,2,1,0:T(8,128)(2,1)}, u32[]{:S(2)}) copy-start(bf16[1,2,128,768]{3,2,1,0:T(8,128)(2,1)} %get-tuple-element.88) | copy-start | bytes 1179652
  35.7 6.9 %copy-start.23 = (s32[2,3]{1,0:T(2,128)S(1)}, s32[2,3]{1,0:T(2,128)}, u32[]{:S(2)}) copy-start(s32[2,3]{1,0:T(2,128)} %copy-done.22) | copy-start | bytes 76
  35.7 10.5 %copy-start.12 = (bf16[256,768]{1,0:T(8,128)(2,1)S(1)}, bf16[256,768]{1,0:T(8,128)(2,1)}, u32[]{:S(2)}) copy-start(bf16[256,768]{1,0:T(8,128)(2,1)} %param.10) | copy-start | bytes 1179652
  35.7 57.5 %all-to-all-start.1 = ((bf16[8,1,2,128,768]{4,3,2,1,0:T(8,128)(2,1)}), bf16[8,1,2,128,768]{4,3,2,1,0:T(8,128)(2,1)}, u32[]{:S(2)}, u32[]{:S(2)}) async-start(bf16[8,1,2,128,768]{4,3,2,1,0:T(8,128)(2,1)} %fusion.10), calls=%async_computation.1 | async-start | bytes 6291456 | tf_op jit(solution)/shard_map/all_to_all | solution.py:78
  40.9 141.4 %all-gather.3.cloned.1.call-start = ((), (), s32[]{:S(2)}) async-start(), calls=%async_computation.5 | async-start | bytes 1966080 | tf_op jit(solution)/shard_map/all_gather | solution.py:103
  40.9 47.0 %collective-permute-start = (bf16[1,2,128,768]{3,2,1,0:T(8,128)(2,1)S(1)}, bf16[1,2,128,768]{3,2,1,0:T(8,128)(2,1)S(1)}, u32[]{:S(2)}, u32[]{:S(2)}) collective-permute-start(bf16[1,2,128,768]{3,2,1,0:T(8,128)(2,1)S(1)} %copy-done.14), channel_id=1, source_target_pairs={{0,4},{4,8},{8,12},{12,16},{16,20},{20,24},{24,28},{28,0},{1,5},{5... | collective-permute-start | bytes 1179656 | tf_op jit(solution)/shard_map/ppermute | solution.py:23
  42.6 48.4 %collective-permute-start.1 = (bf16[1,2,128,768]{3,2,1,0:T(8,128)(2,1)S(1)}, bf16[1,2,128,768]{3,2,1,0:T(8,128)(2,1)S(1)}, u32[]{:S(2)}, u32[]{:S(2)}) collective-permute-start(bf16[1,2,128,768]{3,2,1,0:T(8,128)(2,1)S(1)} %copy-done.13), channel_id=1, source_target_pairs={{4,0},{8,4},{12,8},{16,12},{20,16},{24,20},{28,24},{0,28},{5,1},{9... | collective-permute-start | bytes 1179656 | tf_op jit(solution)/shard_map/ppermute | solution.py:25
  91.9 4.2 %copy-start.16 = (pred[2,3]{1,0:T(4,128)(4,1)S(1)}, pred[2,3]{1,0:T(4,128)(4,1)}, u32[]{:S(2)}) copy-start(pred[2,3]{1,0:T(4,128)(4,1)} %compare_and_fusion.2) | copy-start | bytes 22
  120.3 5.9 %copy-start.9 = (bf16[2,128,6,128]{3,2,1,0:T(8,128)(2,1)S(1)}, bf16[2,128,6,128]{3,2,1,0:T(8,128)(2,1)}, u32[]{:S(2)}) copy-start(bf16[2,128,6,128]{3,2,1,0:T(8,128)(2,1)} %reshape.512) | copy-start | bytes 1179652
  139.2 79.3 %reduce-scatter.3.cloned.1.call-start = ((), (), s32[]{:S(2)}) async-start(), calls=%async_computation.7 | async-start | bytes 1966080 | tf_op jit(solution)/shard_map/reduce_scatter | solution.py:112
  152.2 168.4 %reduce-scatter.5.cloned.1.call-start = ((), (), s32[]{:S(2)}) async-start(), calls=%async_computation.9 | async-start | bytes 10616832 | tf_op jit(solution)/shard_map/reduce_scatter | solution.py:119
  188.8 0.6 copy-start.19
  188.8 0.6 copy-start.21
  235.4 6.8 %copy-start.10 = (bf16[2,128,6,128]{3,2,1,0:T(8,128)(2,1)S(1)}, bf16[2,128,6,128]{3,2,1,0:T(8,128)(2,1)}, u32[]{:S(2)}) copy-start(bf16[2,128,6,128]{3,2,1,0:T(8,128)(2,1)} %reshape.512) | copy-start | bytes 1179652
  240.4 1.8 copy-start.3
  272.6 117.2 %all-to-all-start.2 = ((bf16[8,1,2,128,768]{4,3,2,1,0:T(8,128)(2,1)}), bf16[8,1,2,128,768]{4,3,2,1,0:T(8,128)(2,1)}, u32[]{:S(2)}, u32[]{:S(2)}) async-start(bf16[8,1,2,128,768]{4,3,2,1,0:T(8,128)(2,1)} %fusion.8), calls=%async_computation.3 | async-start | bytes 6291456 | tf_op jit(solution)/shard_map/all_to_all | solution.py:172
  279.1 106.6 %all-reduce.7.cloned.1.call-start = ((), (), s32[]{:S(2)}) async-start(), calls=%async_computation.8 | async-start | bytes 1572864 | tf_op jit(solution)/shard_map/psum | solution.py:159
  320.5 3.5 copy-start.2
  328.4 8.9 %copy-start.4 = (bf16[2,6,128,1024]{2,3,1,0:T(8,128)(2,1)S(1)}, bf16[2,6,128,1024]{2,3,1,0:T(8,128)(2,1)}, u32[]{:S(2)}) copy-start(bf16[2,6,128,1024]{2,3,1,0:T(8,128)(2,1)} %copy-done.3) | copy-start | bytes 9437188
  328.4 8.9 %copy-start.5 = (bf16[2,1024,6,128]{1,3,2,0:T(8,128)(2,1)S(1)}, bf16[2,1024,6,128]{1,3,2,0:T(8,128)(2,1)}, u32[]{:S(2)}) copy-start(bf16[2,1024,6,128]{1,3,2,0:T(8,128)(2,1)} %reshape_squeeze.7) | copy-start | bytes 9437188
  330.6 57.8 %collective-permute-start.2 = (bf16[1,2,128,768]{3,2,1,0:T(8,128)(2,1)S(1)}, bf16[1,2,128,768]{3,2,1,0:T(8,128)(2,1)S(1)}, u32[]{:S(2)}, u32[]{:S(2)}) collective-permute-start(bf16[1,2,128,768]{3,2,1,0:T(8,128)(2,1)S(1)} %get-tuple-element.83), channel_id=1, source_target_pairs={{0,4},{4,8},{8,12},{12,16},{16,20},{20,24},{24,28},{28,0},{1,5},{5... | collective-permute-start | bytes 1179656 | tf_op jit(solution)/shard_map/ppermute | solution.py:23
  339.4 50.2 %collective-permute-start.3 = (bf16[1,2,128,768]{3,2,1,0:T(8,128)(2,1)S(1)}, bf16[1,2,128,768]{3,2,1,0:T(8,128)(2,1)S(1)}, u32[]{:S(2)}, u32[]{:S(2)}) collective-permute-start(bf16[1,2,128,768]{3,2,1,0:T(8,128)(2,1)S(1)} %get-tuple-element.82), channel_id=1, source_target_pairs={{4,0},{8,4},{12,8},{16,12},{20,16},{24,20},{28,24},{0,28},{5,1},{9... | collective-permute-start | bytes 1179656 | tf_op jit(solution)/shard_map/ppermute | solution.py:25
  389.8 3.7 copy-start.18
  393.4 1.4 copy-start.8
  393.5 2.6 copy-start.1
Sparse Core Ops, SparseCore 0:
  16.8 64.3 all-reduce.8
  83.6 60.9 all-gather.4
  146.8 35.4 all-gather.2
  185.0 33.4 reduce-scatter.2
  221.9 98.6 reduce-scatter.4
  325.6 59.9 all-reduce.6
where the time goes:
time: 407 us; the launch traced here: 403 us
  waiting for transfers between devices  185 us (45%)
  local copies, waits for them, and re-layouts  85.9 us (21%)
  matrix products  48.6 us (12%)
  other arithmetic  39 us (10%)
  starting transfers between devices  24.7 us (6%)
  between operations  19.7 us (5%)
    psum x1, waiting for transfers between devices, shards(): lax.psum(global_terms.astype(jnp.bfloat16), 'seq').astype(jnp.float32)  44.7 us
    ppermute x2, waiting for transfers between devices, padded_2(): lax.ppermute(tail, axis, [(i, (i + 1) % count) for i in range(count)])  38.5 us
    reduce_scatter x1, waiting for transfers between devices, shards(): lax.psum_scatter(rounded_grad.astype(jnp.bfloat16), 'seq', scatter_dimens...  33.8 us
    all_gather x1, waiting for transfers between devices, shards(): attended_all = lax.all_gather(attended, 'fsdp', axis=1, tiled=True)  30.1 us
    reduce_scatter x1, waiting for transfers between devices, shards(): lax.psum_scatter(rounded_part.astype(jnp.bfloat16), 'fsdp', scatter_dimen...  28.9 us
    unnamed x59, local copies, waits for them, and re-layouts  22 us
    slice x2, local copies, waits for them, and re-layouts, shards(): key_set = all_kv[:, :, 0].reshape(blocks, NSEL * BLK, heads_here, HD)  11.1 us
    another operation x2, local copies, waits for them, and re-layouts, shards(): jnp.stack([key_terms.reshape(blocks, NSEL, BLK, width_here), value_terms....  8.77 us
  transfers between devices with their start and end apart: 13, of which 7 were waited for; matrix products, arithmetic and copies ran while one was open for 40% of the time, Pallas kernels for 0%

commit v1 on v0

v1 whole, which is shorter than its diff:
```python
import functools
import math

import jax
import jax.numpy as jnp
from jax import lax
from jax.experimental import pallas as pl
from jax.experimental.pallas import tpu as pltpu
from jax.sharding import PartitionSpec as P

HD = 128
BLK = 128
NSEL = 8
MESH = pl.DeviceIdType.MESH
ANY = pl.BlockSpec(memory_space=pl.ANY)
VMEM = pl.BlockSpec(memory_space=pltpu.VMEM)
DMA = pltpu.SemaphoreType.DMA
CHUNK = 32


def remote(src, dst, send_sem, recv_sem, **where):
    return pltpu.make_async_remote_copy(
        src_ref=src,
        dst_ref=dst,
        send_sem=send_sem,
        recv_sem=recv_sem,
        device_id=where,
        device_id_type=MESH,
    )


def chip_place():
    me = lax.axis_index("seq")
    core = lax.rem(me, 2)
    chip = me // 2
    return me, chip, core, chip * 2 + 1 - core


def greet(seq_all, count, fsdp_count):
    me, chip, core, partner = chip_place()
    barrier = pltpu.get_barrier_semaphore()
    total = 0
    if seq_all:
        for k in range(1, count):
            pl.semaphore_signal(
                barrier, inc=1, device_id={"seq": lax.rem(me + k, count)}, device_id_type=MESH
            )
            total += 1
    else:
        pl.semaphore_signal(barrier, inc=1, device_id={"seq": partner}, device_id_type=MESH)
        total += 1
        for k in range(1, count // 2):
            other = lax.rem(chip + k, count // 2) * 2 + core
            pl.semaphore_signal(barrier, inc=1, device_id={"seq": other}, device_id_type=MESH)
            total += 1
    if fsdp_count:
        mine = lax.axis_index("fsdp")
        for k in range(1, fsdp_count):
            other = lax.rem(mine + k, fsdp_count)
            pl.semaphore_signal(barrier, inc=1, device_id={"fsdp": other}, device_id_type=MESH)
            total += 1
    pl.semaphore_wait(barrier, total)


class Gather:
    def __init__(self, count, x, out, send, recv, near_send, near_recv, local):
        self.n = count // 2
        self.x, self.out = x, out
        self.send, self.recv = send, recv
        self.near_send, self.near_recv, self.local = near_send, near_recv, local

    def far(self, k):
        me, chip, core, partner = chip_place()
        other = lax.rem(chip + k, self.n) * 2 + core
        return remote(self.x, self.out.at[me], self.send.at[k], self.recv.at[k], seq=other)

    def near(self, k):
        me, chip, core, partner = chip_place()
        slot = lax.rem(chip + self.n - k, self.n) * 2 + core
        src = self.x if k == 0 else self.out.at[slot]
        return remote(src, self.out.at[slot], self.near_send.at[k], self.near_recv.at[k], seq=partner)

    def start(self):
        me = lax.axis_index("seq")
        for k in range(1, self.n):
            self.far(k).start()
        self.near(0).start()
        self.own = pltpu.make_async_copy(self.x, self.out.at[me], self.local)
        self.own.start()

    def forward(self):
        for k in range(1, self.n):
            self.far(k).wait_recv()
            self.near(k).start()

    def finish(self):
        self.own.wait()
        for k in range(1, self.n):
            self.far(k).wait_send()
        for k in range(self.n):
            self.near(k).wait_send()
            self.near(k).wait_recv()


class Scatter:
    def __init__(self, count, x, out, got, staged, arrived, send, recv, near_send, near_recv):
        self.n = count // 2
        self.x, self.out, self.got, self.staged, self.arrived = x, out, got, staged, arrived
        self.send, self.recv, self.near_send, self.near_recv = send, recv, near_send, near_recv

    def near(self, k):
        me, chip, core, partner = chip_place()
        slot = lax.rem(chip + k, self.n) * 2 + 1 - core
        return remote(
            self.x.at[slot], self.got.at[k], self.near_send.at[k], self.near_recv.at[k], seq=partner
        )

    def far(self, k):
        me, chip, core, partner = chip_place()
        other = lax.rem(chip + k, self.n) * 2 + core
        return remote(
            self.staged.at[k], self.arrived.at[k], self.send.at[k], self.recv.at[k], seq=other
        )

    def start(self):
        for k in list(range(1, self.n)) + [0]:
            self.near(k).start()

    def exchange(self, k):
        me, chip, core, partner = chip_place()
        slot = lax.rem(chip + k, self.n) * 2 + core
        self.near(k).wait_recv()

        def body(i, carry):
            rows = pl.ds(pl.multiple_of(i * CHUNK, CHUNK), CHUNK)
            total = self.x[slot, rows, :].astype(jnp.float32) + self.got[k, rows, :].astype(
                jnp.float32
            )
            self.staged[k, rows, :] = total.astype(jnp.bfloat16)
            return carry

        lax.fori_loop(0, self.x.shape[1] // CHUNK, body, 0)
        if k:
            self.far(k).start()

    def finish(self):
        for k in range(1, self.n):
            self.far(k).wait_recv()

        def body(i, carry):
            rows = pl.ds(pl.multiple_of(i * CHUNK, CHUNK), CHUNK)
            total = self.staged[0, rows, :].astype(jnp.float32)
            for k in range(1, self.n):
                total = total + self.arrived[k, rows, :].astype(jnp.float32)
            self.out[rows, :] = total.astype(jnp.bfloat16)
            return carry

        lax.fori_loop(0, self.x.shape[1] // CHUNK, body, 0)
        for k in range(1, self.n):
            self.far(k).wait_send()
        for k in range(self.n):
            self.near(k).wait_send()


def gather_sems(n):
    return [DMA((n,)), DMA((n,)), DMA((n,)), DMA((n,)), DMA]


def scatter_scratch(count, shape):
    n = count // 2
    buffers = [pltpu.VMEM((n,) + shape, jnp.bfloat16) for unused in range(3)]
    return buffers + [DMA((n,)), DMA((n,)), DMA((n,)), DMA((n,))]


def params(number, mib=48):
    return pltpu.CompilerParams(
        collective_id=number, has_side_effects=True, vmem_limit_bytes=mib * 2**20
    )


def gather_kernel(count, x, out, *sems):
    greet(False, count, 0)
    work = Gather(count, x, out, *sems)
    work.start()
    work.forward()
    work.finish()


def gather_grad(count, out_grad):
    return pl.pallas_call(
        functools.partial(gather_kernel, count),
        out_shape=jax.ShapeDtypeStruct((count,) + out_grad.shape, out_grad.dtype),
        in_specs=[ANY],
        out_specs=ANY,
        scratch_shapes=gather_sems(count // 2),
        compiler_params=params(1, 16),
        name="gather_out_grad",
    )(out_grad)


def middle_kernel(count, fs, k_ref, v_ref, part_ref, k_out, v_out, head_out, *scratch):
    k_sems, v_sems = scratch[:5], scratch[5:10]
    parts, summed, z_send, z_recv, s_send, s_recv, local = scratch[10:]
    me = lax.axis_index("seq")
    mine = lax.axis_index("fsdp")
    greet(True, count, fs)

    def z_copy(k):
        other = lax.rem(mine + k, fs)
        return remote(part_ref.at[other], parts.at[k], z_send.at[k], z_recv.at[k], fsdp=other)

    def s_copy(k):
        other = lax.rem(me + k, count)
        return remote(summed.at[other], head_out.at[me], s_send.at[k], s_recv.at[k], seq=other)

    for k in range(1, fs):
        z_copy(k).start()
    works = [Gather(count, k_ref, k_out, *k_sems), Gather(count, v_ref, v_out, *v_sems)]
    for work in works:
        work.start()
    for k in range(1, fs):
        z_copy(k).wait_recv()

    def body(j, carry):
        total = part_ref[mine, j].astype(jnp.float32)
        for k in range(1, fs):
            total = total + parts[k, j].astype(jnp.float32)
        summed[j] = total.astype(jnp.bfloat16)
        return carry

    lax.fori_loop(0, count, body, 0)
    for k in range(1, count):
        s_copy(k).start()
    own = pltpu.make_async_copy(summed.at[me], head_out.at[me], local)
    own.start()
    for work in works:
        work.forward()
    for work in works:
        work.finish()
    own.wait()
    for k in range(1, fs):
        z_copy(k).wait_send()
    for k in range(1, count):
        s_copy(k).wait()


def middle(count, fs, key_rows, value_rows, part):
    slots = part.shape[1:]
    return pl.pallas_call(
        functools.partial(middle_kernel, count, fs),
        out_shape=[
            jax.ShapeDtypeStruct((count,) + key_rows.shape, jnp.bfloat16),
            jax.ShapeDtypeStruct((count,) + key_rows.shape, jnp.bfloat16),
            jax.ShapeDtypeStruct(slots, jnp.bfloat16),
        ],
        in_specs=[ANY, ANY, VMEM],
        out_specs=[ANY, ANY, ANY],
        scratch_shapes=gather_sems(count // 2)
        + gather_sems(count // 2)
        + [
            pltpu.VMEM((fs,) + slots, jnp.bfloat16),
            pltpu.VMEM(slots, jnp.bfloat16),
            DMA((fs,)),
            DMA((fs,)),
            DMA((count,)),
            DMA((count,)),
            DMA,
        ],
        compiler_params=params(2),
        name="gather_keys_values_sum_head_grad",
    )(key_rows, value_rows, part)


def attend_kernel(blocks, pat, q_ref, k_ref, v_ref, g_ref, att_ref, qg_ref, kg_ref, vg_ref, *scratch):
    k_set, v_set, k_acc, v_acc = scratch
    scale = 1.0 / math.sqrt(HD)
    f32, low = jnp.float32, jnp.bfloat16
    k_acc[...] = jnp.zeros_like(k_acc)
    v_acc[...] = jnp.zeros_like(v_acc)
    nt = (((1,), (1,)), ((), ()))
    nn = (((1,), (0,)), ((), ()))
    tn = (((0,), (0,)), ((), ()))

    def dot(a, b, dims):
        return lax.dot_general(a, b, dims, preferred_element_type=f32)

    for j in range(blocks):
        here = slice(j * BLK, (j + 1) * BLK)
        for s in range(NSEL):
            at = pl.ds(pl.multiple_of(pat[j, s] * BLK, BLK), BLK)
            k_set[s * BLK : (s + 1) * BLK, :] = k_ref[at, :]
            v_set[s * BLK : (s + 1) * BLK, :] = v_ref[at, :]
        q = q_ref[here, :]
        g = g_ref[:, here]
        scores = dot(k_set[...], q, nt) * scale
        top = jnp.max(scores, axis=0, keepdims=True)
        exps = jnp.exp(scores - top)
        probs = exps * (1.0 / jnp.sum(exps, axis=0, keepdims=True))
        probs_low = probs.astype(low)
        att_ref[:, here] = dot(v_set[...], probs_low, tn).astype(low)
        prob_grad = dot(v_set[...], g, nn)
        center = jnp.sum(probs * prob_grad, axis=0, keepdims=True)
        score_grad = (probs * (prob_grad - center)).astype(low)
        qg_ref[here, :] = (dot(score_grad, k_set[...], tn) * scale).astype(low)
        k_term = (dot(score_grad, q, nn) * scale).astype(low)
        v_term = dot(probs_low, g, nt).astype(low)
        for s in range(NSEL):
            at = pl.ds(pl.multiple_of(pat[j, s] * BLK, BLK), BLK)
            k_acc[at, :] += k_term[s * BLK : (s + 1) * BLK, :].astype(f32)
            v_acc[at, :] += v_term[s * BLK : (s + 1) * BLK, :].astype(f32)
    kg_ref[...] = k_acc[...].astype(low)
    vg_ref[...] = v_acc[...].astype(low)


def attend(pattern, queries, keys, values, grad_t):
    rows, width = queries.shape
    tokens = keys.shape[0]
    low = jnp.bfloat16
    by_col = lambda n: pl.BlockSpec((n, HD), lambda h, pat: (0, h))
    by_row = pl.BlockSpec((HD, rows), lambda h, pat: (h, 0))
    return pl.pallas_call(
        functools.partial(attend_kernel, rows // BLK),
        grid_spec=pltpu.PrefetchScalarGridSpec(
            num_scalar_prefetch=1,
            grid=(width // HD,),
            in_specs=[by_col(rows), by_col(tokens), by_col(tokens), by_row],
            out_specs=[by_row, by_col(rows), by_col(tokens), by_col(tokens)],
            scratch_shapes=[
                pltpu.VMEM((NSEL * BLK, HD), low),
                pltpu.VMEM((NSEL * BLK, HD), low),
                pltpu.VMEM((tokens, HD), jnp.float32),
                pltpu.VMEM((tokens, HD), jnp.float32),
            ],
        ),
        out_shape=[
            jax.ShapeDtypeStruct((width, rows), low),
            jax.ShapeDtypeStruct((rows, width), low),
            jax.ShapeDtypeStruct((tokens, width), low),
            jax.ShapeDtypeStruct((tokens, width), low),
        ],
        compiler_params=pltpu.CompilerParams(vmem_limit_bytes=48 * 2**20),
        name="attend",
    )(pattern, queries, keys, values, grad_t)


def late_kernel(count, fs, kg_ref, vg_ref, att_ref, k_out, v_out, att_out, *scratch):
    k_scratch, v_scratch = scratch[:7], scratch[7:14]
    s_send, s_recv, z_send, z_recv, local = scratch[14:]
    me = lax.axis_index("seq")
    mine = lax.axis_index("fsdp")
    greet(True, count, fs)

    def s_copy(k):
        other = lax.rem(me + k, count)
        return remote(
            att_ref.at[other], att_out.at[mine, me], s_send.at[k], s_recv.at[k], seq=other
        )

    def z_copy(k):
        other = lax.rem(mine + k, fs)
        return remote(att_out.at[mine], att_out.at[mine], z_send.at[k], z_recv.at[k], fsdp=other)

    for k in range(1, count):
        s_copy(k).start()
    own = pltpu.make_async_copy(att_ref.at[me], att_out.at[mine, me], local)
    own.start()
    works = [
        Scatter(count, kg_ref, k_out, *k_scratch),
        Scatter(count, vg_ref, v_out, *v_scratch),
    ]
    for work in works:
        work.start()
    own.wait()
    for k in range(1, count):
        s_copy(k).wait_recv()
    for k in range(1, fs):
        z_copy(k).start()
    for k in list(range(1, count // 2)) + [0]:
        for work in works:
            work.exchange(k)
    for work in works:
        work.finish()
    for k in range(1, count):
        s_copy(k).wait_send()
    for k in range(1, fs):
        z_copy(k).wait()


def late(count, fs, key_sums, value_sums, att):
    shape = key_sums.shape[1:]
    return pl.pallas_call(
        functools.partial(late_kernel, count, fs),
        out_shape=[
            jax.ShapeDtypeStruct(shape, jnp.bfloat16),
            jax.ShapeDtypeStruct(shape, jnp.bfloat16),
            jax.ShapeDtypeStruct((fs,) + att.shape, jnp.bfloat16),
        ],
        in_specs=[VMEM, VMEM, ANY],
        out_specs=[VMEM, VMEM, ANY],
        scratch_shapes=scatter_scratch(count, shape)
        + scatter_scratch(count, shape)
        + [DMA((count,)), DMA((count,)), DMA((fs,)), DMA((fs,)), DMA],
        compiler_params=params(3, 56),
        name="sum_key_value_grads_gather_attended",
    )(key_sums, value_sums, att)


def scatter_kernel(count, x, out, *scratch):
    greet(False, count, 0)
    work = Scatter(count, x, out, *scratch)
    work.start()
    for k in list(range(1, count // 2)) + [0]:
        work.exchange(k)
    work.finish()


def scatter_projected(count, partial):
    shape = partial.shape[1:]
    return pl.pallas_call(
        functools.partial(scatter_kernel, count),
        out_shape=jax.ShapeDtypeStruct(shape, jnp.bfloat16),
        in_specs=[VMEM],
        out_specs=VMEM,
        scratch_shapes=scatter_scratch(count, shape),
        compiler_params=params(4, 56),
        name="sum_projected",
    )(partial)


def shards(count, fs, queries, key_rows, value_rows, pattern, out_weight, out_grad):
    rows, width = queries.shape
    heads = width // HD
    part_e, heads_all, cols = out_weight.shape
    tokens = rows * count
    f32, low = jnp.float32, jnp.bfloat16
    weight = out_weight.reshape(part_e * heads_all, cols)

    grad_all = gather_grad(count, out_grad).reshape(tokens, cols)
    head_part = lax.dot_general(
        weight, grad_all, (((1,), (1,)), ((), ())), preferred_element_type=f32
    ).astype(low)
    head_part = head_part.reshape(part_e, fs, heads, count, rows)
    head_part = head_part.transpose(1, 3, 0, 2, 4).reshape(fs, count, part_e * heads, rows)

    keys, values, head_grad = middle(count, fs, key_rows, value_rows, head_part)
    grad_t = head_grad.reshape(count, part_e, heads, rows).transpose(2, 0, 1, 3)
    att_t, query_grad, key_sums, value_sums = attend(
        pattern,
        queries,
        keys.reshape(tokens, width),
        values.reshape(tokens, width),
        grad_t.reshape(width, rows),
    )
    att = att_t.reshape(heads, count, part_e, rows).transpose(1, 2, 0, 3)
    key_grad, value_grad, att_all = late(
        count,
        fs,
        key_sums.reshape(count, rows, width),
        value_sums.reshape(count, rows, width),
        att.reshape(count, part_e * heads, rows),
    )
    att_all = att_all.reshape(fs, count, part_e, heads, rows).transpose(2, 0, 3, 1, 4)
    att_all = att_all.reshape(part_e * heads_all, tokens)
    partial = lax.dot_general(
        att_all, weight, (((0,), (0,)), ((), ())), preferred_element_type=f32
    ).astype(low)
    projected = scatter_projected(count, partial.reshape(count, rows, cols))
    weight_grad = lax.dot_general(
        att_all, grad_all, (((1,), (0,)), ((), ())), preferred_element_type=f32
    ).reshape(part_e, heads_all, cols)
    return (projected, query_grad, key_grad, value_grad, weight_grad)


def solution(mesh):
    placed = (
        P("seq", "fsdp"),
        P("seq", "fsdp"),
        P("seq", "fsdp"),
        P("seq", None),
        P("seq", None, "fsdp"),
        P("seq", "fsdp"),
    )
    return jax.shard_map(
        functools.partial(shards, mesh.shape["seq"], mesh.shape["fsdp"]),
        mesh=mesh,
        in_specs=placed,
        out_specs=(
            P("seq", "fsdp"),
            P("seq", "fsdp"),
            P("seq", "fsdp"),
            P("seq", "fsdp"),
            P("seq", None, "fsdp"),
        ),
        check_vma=False,
    )
```

time: 407 us -> 233 us (0.57)
  Pallas kernels: 0 us -> 195 us
  waiting for transfers between devices: 185 us -> 0 us
  local copies, waits for them, and re-layouts: 85.9 us -> 18.6 us
  other arithmetic: 39 us -> 0 us
  matrix products: 48.6 us -> 15.4 us
  starting transfers between devices: 24.7 us -> 0 us
  between operations: 19.7 us -> 0.81 us
    pallas_call x0 -> x5, Pallas kernels: none -> 195 us  [the longest x1 48.8 us: late(): pl.pallas_call(functools.partial(late_kernel, count, fs), out_shape=[jax....]
    reduce_scatter x2 -> x0, waiting for transfers between devices: 62.7 us -> none  [the longest x1 33.8 us: shards(): lax.psum_scatter(rounded_grad.astype(jnp.bfloat16), 'seq', scatter_dimens...]
    psum x2 -> x0, waiting for transfers between devices: 44.7 us -> none  [the longest x1 44.7 us: shards(): lax.psum(global_terms.astype(jnp.bfloat16), 'seq').astype(jnp.float32)]
    ppermute x4 -> x0, waiting for transfers between devices: 38.5 us -> none  [the longest x2 38.5 us: padded_2(): lax.ppermute(tail, axis, [(i, (i + 1) % count) for i in range(count)])]
    all_gather x2 -> x0, waiting for transfers between devices: 35.3 us -> none  [the longest x1 30.1 us: shards(): attended_all = lax.all_gather(attended, 'fsdp', axis=1, tiled=True)]
    dot_general x9 -> x3, matrix products: 41.5 us -> 15.4 us  [the longest x1 7.39 us: shards(): lax.dot_general(att_all, grad_all, (((1,), (0,)), ((), ())), preferred_el...]
    slice x9 -> x0, local copies, waits for them, and re-layouts: 21.9 us -> none  [the longest x2 11.1 us: shards(): key_set = all_kv[:, :, 0].reshape(blocks, NSEL * BLK, heads_here, HD)]
    another operation x4 -> x0, local copies, waits for them, and re-layouts: 20.4 us -> none  [the longest x2 8.77 us: shards(): jnp.stack([key_terms.reshape(blocks, NSEL, BLK, width_here), value_terms....]
  transfers between devices with their start and end apart: 13 -> 0, of which waited for: 7 -> 0; matrix products, arithmetic and copies ran while one was open for 40% -> 0% of each run, Pallas kernels for 0% -> 0%
where the time goes in v1:
time: 233 us; the launch traced here: 230 us
  Pallas kernels  195 us (84%)
  local copies, waits for them, and re-layouts  18.6 us (8%)
  matrix products  15.4 us (7%)
    pallas_call x1, Pallas kernels, late(): pl.pallas_call(functools.partial(late_kernel, count, fs), out_shape=[jax....  48.8 us
    pallas_call x1, Pallas kernels, middle(): pl.pallas_call(functools.partial(middle_kernel, count, fs), out_shape=[ja...  44.3 us
    pallas_call x1, Pallas kernels, scatter_projected(): pl.pallas_call(functools.partial(scatter_kernel, count), out_shape=jax.Sh...  44.3 us
    pallas_call x1, Pallas kernels, gather_grad(): pl.pallas_call(functools.partial(gather_kernel, count), out_shape=jax.Sha...  40.8 us
    pallas_call x1, Pallas kernels, attend(): pl.pallas_call(functools.partial(attend_kernel, rows // BLK), grid_spec=p...  17.2 us
    unnamed x29, local copies, waits for them, and re-layouts  12.2 us
    dot_general x1, matrix products, shards(): lax.dot_general(att_all, grad_all, (((1,), (0,)), ((), ())), preferred_el...  7.39 us
    dot_general x1, matrix products, shards(): lax.dot_general(att_all, weight, (((0,), (0,)), ((), ())), preferred_elem...  5.35 us

profile of v1, /device:TPU:9, one launch (start us, length us, event | category | flops | bytes accessed | tf_op | source)
XLA Modules:
  0.0 230.1 jit_solution(4468201054310181381)
XLA Ops:
  0.6 0.0 copy-start
  0.6 1.3 copy-done
  1.9 0.0 copy-start.4
  1.9 1.1 copy-done.4
  3.0 40.8 %gather_out_grad.1 = bf16[8,256,1536]{2,1,0:T(8,128)(2,1)S(1)} custom-call(bf16[256,1536]{1,0:T(8,128)(2,1)S(1)} %copy-done.4), custom_call_target="tpu_custom_call" | custom-call | tf_op jit(solution)/shard_map/gather_out_grad/pallas_call | solution.py:190
  43.9 0.0 copy-start.1
  43.9 2.6 %convolution_convert_fusion.1 = bf16[384,2048]{1,0:T(8,128)(2,1)S(1)} fusion(bf16[384,1536]{1,0:T(8,128)(2,1)S(1)} %bitcast.37, bf16[2048,1536]{1,0:T(8,128)(2,1)S(1)} %bitcast.39), kind=kOutput, calls=%fused_computation.1 | convolution fusion | flops 2416705536 | bytes 9043968 | tf_op jit(solution)/shard_map/dot_general | solution.py:439
  46.5 0.0 copy-done.1
  46.6 0.5 copy.32
  47.0 0.1 copy.23
  47.2 0.0 copy-start.5
  47.2 0.0 copy-start.6
  47.2 0.4 copy.24.part_ref
  47.6 0.6 copy-done.5
  48.2 0.1 copy-done.6
  48.3 0.0 copy-start.7
  48.3 0.0 copy-start.8
  48.3 44.3 %gather_keys_values_sum_head_grad.1 = (bf16[8,256,768]{2,1,0:T(8,128)(2,1)S(1)}, bf16[8,256,768]{2,1,0:T(8,128)(2,1)}, bf16[8,96,256]{2,1,0:T(8,128)(2,1)S(1)}) custom-call(bf16[256,768]{1,0:T(8,128)(2,1)S(1)} %copy-done.5, bf16[256,768]{1,0:T(8,128)(2,1)S(1)} %copy-done.6, bf16[4,8,96,256]{3,2,1,0:T(8,128)(2,1)S(1)} %copy.24.part_ref), custom_call_target="tpu_custom_call" | custom-call | tf_op jit(solution)/shard_map/gather_keys_values_sum_head_grad/pallas_call | solution.py:249
  92.6 0.0 copy-start.3
  92.6 1.6 copy-done.3
  94.3 0.2 copy.25
  94.5 0.1 copy.26
  94.6 0.0 copy-done.7
  94.6 0.0 copy-done.8
  94.6 17.2 %attend.1 = (bf16[768,256]{1,0:T(8,128)(2,1)S(1)}, bf16[256,768]{1,0:T(8,128)(2,1)}, bf16[2048,768]{1,0:T(8,128)(2,1)S(1)}, bf16[2048,768]{1,0:T(8,128)(2,1)}) custom-call(s32[2,8]{1,0:T(2,128)S(1)} %copy-done.8, bf16[256,768]{1,0:T(8,128)(2,1)S(1)} %copy-done.7, bf16[2048,768]{1,0:T(8,128)(2,1)} %bitcast.42, bf16[2048,768]{1,0:T(8,128)(2,1)} %bitcast.51, ...), custom_call_target="tpu_custom_call" | custom-call | tf_op jit(solution)/shard_map/attend/pallas_call | solution.py:321
  111.8 0.0 copy-start.2
  111.8 1.6 copy-done.2
  113.4 0.1 copy.27
  113.6 0.8 copy.28.att_ref
  114.4 48.8 %sum_key_value_grads_gather_attended.1 = (bf16[256,768]{1,0:T(8,128)(2,1)}, bf16[256,768]{1,0:T(8,128)(2,1)}, bf16[4,8,96,256]{3,2,1,0:T(8,128)(2,1)}) custom-call(bf16[8,256,768]{2,1,0:T(8,128)(2,1)} %bitcast.41, bf16[8,256,768]{2,1,0:T(8,128)(2,1)} %bitcast.50, bf16[8,96,256]{2,1,0:T(8,128)(2,1)} %copy.28.att_ref), custom_call_target="tpu_custom_call" | custom-call | tf_op jit(solution)/shard_map/sum_key_value_grads_gather_attended/pallas_call | solution.py:391
  163.2 2.3 copy.29
  165.5 0.1 copy.30
  165.6 1.7 copy.33
  167.3 2.1 dot_general.13
  169.4 0.0 copy-start.9
  169.4 7.4 %fusion = f32[16,24,1536]{2,1,0:T(8,128)} fusion(bf16[16,24,2048]{2,1,0:T(8,128)(2,1)} %dot_general.13, bf16[2048,1536,1]{1,0,2:T(8,128)(2,1)} %bitcast.40), kind=kOutput, calls=%fused_computation.2 | convolution fusion | flops 2415919104 | bytes 10223616 | tf_op jit(solution)/shard_map/dot_general | solution.py:468
  176.8 0.0 copy-done.9
  176.8 5.3 %convolution_convert_fusion = bf16[2048,1536]{1,0:T(8,128)(2,1)} fusion(bf16[384,2048]{1,0:T(8,128)(2,1)S(1)} %bitcast.52, bf16[384,1536]{1,0:T(8,128)(2,1)S(1)} %bitcast.38), kind=kOutput, calls=%fused_computation | convolution fusion | flops 2419064832 | bytes 9043968 | tf_op jit(solution)/shard_map/dot_general | solution.py:464
  182.2 44.3 %sum_projected.1 = bf16[256,1536]{1,0:T(8,128)(2,1)} custom-call(bf16[8,256,1536]{2,1,0:T(8,128)(2,1)} %bitcast.46), custom_call_target="tpu_custom_call" | custom-call | tf_op jit(solution)/shard_map/sum_projected/pallas_call | solution.py:419
  226.4 0.0 copy-start.11
  226.5 0.0 copy-start.10
  226.5 2.1 copy.37
  228.6 0.0 copy-done.11
  228.6 0.7 copy.38
  229.3 0.0 copy-done.10
  229.3 0.7 copy.39
Async XLA Ops:
  0.6 1.3 copy-start
  1.9 1.1 copy-start.4
  43.9 2.6 %copy-start.1 = (bf16[8,256,1536]{2,1,0:T(8,128)(2,1)}, bf16[8,256,1536]{2,1,0:T(8,128)(2,1)S(1)}, u32[]{:S(2)}) copy-start(bf16[8,256,1536]{2,1,0:T(8,128)(2,1)S(1)} %gather_out_grad.1) | copy-start | bytes 18874372
  47.2 1.0 copy-start.5
  47.2 1.1 copy-start.6
  48.3 46.3 %copy-start.7 = (bf16[256,768]{1,0:T(8,128)(2,1)S(1)}, bf16[256,768]{1,0:T(8,128)(2,1)}, u32[]{:S(2)}) copy-start(bf16[256,768]{1,0:T(8,128)(2,1)} %q_ref.1) | copy-start | bytes 1179652
  48.3 46.3 %copy-start.8 = (s32[2,8]{1,0:T(2,128)S(1)}, s32[2,8]{1,0:T(2,128)}, u32[]{:S(2)}) copy-start(s32[2,8]{1,0:T(2,128)} %pat.1) | copy-start | bytes 196
  92.6 1.6 copy-start.3
  111.8 1.7 copy-start.2
  169.4 7.4 %copy-start.9 = (bf16[48,8,8,256]{3,1,2,0:T(8,128)(2,1)S(1)}, bf16[48,8,8,256]{3,1,2,0:T(8,128)(2,1)}, u32[]{:S(2)}) copy-start(bf16[48,8,8,256]{3,1,2,0:T(8,128)(2,1)} %copy.33) | copy-start | bytes 4718596
  226.4 2.2 copy-start.11
  226.5 2.9 %copy-start.10 = (bf16[256,768]{1,0:T(8,128)(2,1)S(1)}, bf16[256,768]{1,0:T(8,128)(2,1)}, u32[]{:S(2)}) copy-start(bf16[256,768]{1,0:T(8,128)(2,1)} %get-tuple-element.33) | copy-start | bytes 1179652

commit v2 on v1

--- a/solution.py
+++ b/solution.py
@@ -62,43 +62,73 @@
     pl.semaphore_wait(barrier, total)
 
 
+def chips(n):
+    me, chip, core, partner = chip_place()
+    if n != 4:
+        there = [lax.rem(chip + k, n) for k in range(n)]
+        return there, [lax.rem(chip + n - k, n) for k in range(n)]
+    x, y = lax.rem(chip, 2), chip // 2
+    beside, across = y * 2 + 1 - x, (1 - y) * 2 + x
+    first = beside + core * (across - beside)
+    second = across + core * (beside - across)
+    return [chip, first, second, second], [chip, first, second, 3 - chip]
+
+
+def mate(n, k):
+    return 3 - k if n == 4 and k in (1, 2) else k
+
+
 class Gather:
     def __init__(self, count, x, out, send, recv, near_send, near_recv, local):
         self.n = count // 2
         self.x, self.out = x, out
         self.send, self.recv = send, recv
         self.near_send, self.near_recv, self.local = near_send, near_recv, local
+        self.me, self.chip, self.core, self.partner = chip_place()
+        self.there, self.source = chips(self.n)
+
+    def relayed(self, k):
+        return self.n == 4 and k == 3
 
     def far(self, k):
-        me, chip, core, partner = chip_place()
-        other = lax.rem(chip + k, self.n) * 2 + core
-        return remote(self.x, self.out.at[me], self.send.at[k], self.recv.at[k], seq=other)
+        src, slot = self.x, self.me
+        if self.relayed(k):
+            slot = self.source[1] * 2 + self.core
+            src = self.out.at[slot]
+        other = self.there[k] * 2 + self.core
+        return remote(src, self.out.at[slot], self.send.at[k], self.recv.at[k], seq=other)
 
     def near(self, k):
-        me, chip, core, partner = chip_place()
-        slot = lax.rem(chip + self.n - k, self.n) * 2 + core
+        slot = self.source[k] * 2 + self.core
         src = self.x if k == 0 else self.out.at[slot]
-        return remote(src, self.out.at[slot], self.near_send.at[k], self.near_recv.at[k], seq=partner)
+        return remote(
+            src, self.out.at[slot], self.near_send.at[k], self.near_recv.at[k], seq=self.partner
+        )
 
     def start(self):
-        me = lax.axis_index("seq")
         for k in range(1, self.n):
-            self.far(k).start()
+            if not self.relayed(k):
+                self.far(k).start()
         self.near(0).start()
-        self.own = pltpu.make_async_copy(self.x, self.out.at[me], self.local)
+        self.own = pltpu.make_async_copy(self.x, self.out.at[self.me], self.local)
         self.own.start()
 
-    def forward(self):
-        for k in range(1, self.n):
-            self.far(k).wait_recv()
-            self.near(k).start()
-
-    def finish(self):
-        self.own.wait()
+    def arrive(self, k):
+        self.far(k).wait_recv()
+        if k == 1 and self.n == 4:
+            self.far(3).start()
+        self.near(k).start()
+
+    def finish_far(self):
         for k in range(1, self.n):
             self.far(k).wait_send()
         for k in range(self.n):
             self.near(k).wait_send()
+
+    def finish(self):
+        self.own.wait()
+        self.finish_far()
+        for k in range(self.n):
             self.near(k).wait_recv()
 
 
@@ -107,35 +137,55 @@
         self.n = count // 2
         self.x, self.out, self.got, self.staged, self.arrived = x, out, got, staged, arrived
         self.send, self.recv, self.near_send, self.near_recv = send, recv, near_send, near_recv
+        self.me, self.chip, self.core, self.partner = chip_place()
+        self.there, self.source = chips(self.n)
+        self.relay = self.n == 4
+        self.dest = self.source if self.relay else self.there
+        self.order = [3, 1, 2, 0] if self.relay else list(range(1, self.n)) + [0]
+
+    def near_slot(self, k):
+        return self.dest[mate(self.n, k)] * 2 + 1 - self.core
+
+    def own_slot(self, k):
+        return self.dest[k] * 2 + self.core
 
     def near(self, k):
-        me, chip, core, partner = chip_place()
-        slot = lax.rem(chip + k, self.n) * 2 + 1 - core
         return remote(
-            self.x.at[slot], self.got.at[k], self.near_send.at[k], self.near_recv.at[k], seq=partner
+            self.x.at[self.near_slot(k)],
+            self.got.at[k],
+            self.near_send.at[k],
+            self.near_recv.at[k],
+            seq=self.partner,
         )
 
     def far(self, k):
-        me, chip, core, partner = chip_place()
-        other = lax.rem(chip + k, self.n) * 2 + core
+        chip = self.there[1] if self.relay and k == 3 else self.there[k]
         return remote(
-            self.staged.at[k], self.arrived.at[k], self.send.at[k], self.recv.at[k], seq=other
+            self.staged.at[k],
+            self.arrived.at[k],
+            self.send.at[k],
+            self.recv.at[k],
+            seq=chip * 2 + self.core,
         )
 
     def start(self):
-        for k in list(range(1, self.n)) + [0]:
+        for k in self.order:
             self.near(k).start()
 
     def exchange(self, k):
-        me, chip, core, partner = chip_place()
-        slot = lax.rem(chip + k, self.n) * 2 + core
+        slot = self.own_slot(k)
         self.near(k).wait_recv()
+        hop = self.relay and k == 2
+        if hop:
+            self.far(3).wait_recv()
 
         def body(i, carry):
             rows = pl.ds(pl.multiple_of(i * CHUNK, CHUNK), CHUNK)
             total = self.x[slot, rows, :].astype(jnp.float32) + self.got[k, rows, :].astype(
                 jnp.float32
             )
+            if hop:
+                total = total + self.arrived[3, rows, :].astype(jnp.float32)
             self.staged[k, rows, :] = total.astype(jnp.bfloat16)
             return carry
 
@@ -144,13 +194,14 @@
             self.far(k).start()
 
     def finish(self):
-        for k in range(1, self.n):
+        last = [1, 2] if self.relay else list(range(1, self.n))
+        for k in last:
             self.far(k).wait_recv()
 
         def body(i, carry):
             rows = pl.ds(pl.multiple_of(i * CHUNK, CHUNK), CHUNK)
             total = self.staged[0, rows, :].astype(jnp.float32)
-            for k in range(1, self.n):
+            for k in last:
                 total = total + self.arrived[k, rows, :].astype(jnp.float32)
             self.out[rows, :] = total.astype(jnp.bfloat16)
             return carry
@@ -178,51 +229,68 @@
     )
 
 
-def gather_kernel(count, x, out, *sems):
-    greet(False, count, 0)
-    work = Gather(count, x, out, *sems)
-    work.start()
-    work.forward()
-    work.finish()
-
-
-def gather_grad(count, out_grad):
-    return pl.pallas_call(
-        functools.partial(gather_kernel, count),
-        out_shape=jax.ShapeDtypeStruct((count,) + out_grad.shape, out_grad.dtype),
-        in_specs=[ANY],
-        out_specs=ANY,
-        scratch_shapes=gather_sems(count // 2),
-        compiler_params=params(1, 16),
-        name="gather_out_grad",
-    )(out_grad)
-
-
-def middle_kernel(count, fs, k_ref, v_ref, part_ref, k_out, v_out, head_out, *scratch):
-    k_sems, v_sems = scratch[:5], scratch[5:10]
-    parts, summed, z_send, z_recv, s_send, s_recv, local = scratch[10:]
+def first_kernel(count, fs, grad_ref, w_ref, k_ref, v_ref, grad_out, k_out, v_out, head_out, *scratch):
+    n = count // 2
+    grad = Gather(count, grad_ref, grad_out, *scratch[:5])
+    works = [
+        Gather(count, k_ref, k_out, *scratch[5:10]),
+        Gather(count, v_ref, v_out, *scratch[10:15]),
+    ]
+    part, parts, summed, z_send, z_recv, s_send, s_recv, local = scratch[15:]
     me = lax.axis_index("seq")
     mine = lax.axis_index("fsdp")
+    rows = w_ref.shape[0] // fs
     greet(True, count, fs)
 
-    def z_copy(k):
+    def z_copy(k, step):
         other = lax.rem(mine + k, fs)
-        return remote(part_ref.at[other], parts.at[k], z_send.at[k], z_recv.at[k], fsdp=other)
+        pair = pl.ds(grad.source[step] * 2, 2)
+        at = k * n + step
+        return remote(
+            part.at[other, pair], parts.at[k, pair], z_send.at[at], z_recv.at[at], fsdp=other
+        )
 
     def s_copy(k):
         other = lax.rem(me + k, count)
         return remote(summed.at[other], head_out.at[me], s_send.at[k], s_recv.at[k], seq=other)
 
+    def multiply(step):
+        for half in range(2):
+            slot = grad.source[step] * 2 + half
+            product = lax.dot_general(
+                w_ref[...],
+                grad_out[slot],
+                (((1,), (1,)), ((), ())),
+                preferred_element_type=jnp.float32,
+            )
+            for f in range(fs):
+                part[f, slot] = product[f * rows : (f + 1) * rows].astype(jnp.bfloat16)
+        for k in range(1, fs):
+            z_copy(k, step).start()
+
+    grad.start()
+    grad.own.wait()
+    grad.near(0).wait_recv()
+    multiply(0)
+    for k in range(1, n):
+        grad.arrive(k)
+        if k == n - 1:
+            for work in works:
+                work.start()
+        if k > 1:
+            grad.near(mate(n, k - 1)).wait_recv()
+            multiply(k - 1)
+    grad.near(n - 1).wait_recv()
+    multiply(n - 1)
+    for k in range(1, n - 1):
+        for work in works:
+            work.arrive(k)
     for k in range(1, fs):
-        z_copy(k).start()
-    works = [Gather(count, k_ref, k_out, *k_sems), Gather(count, v_ref, v_out, *v_sems)]
-    for work in works:
-        work.start()
-    for k in range(1, fs):
-        z_copy(k).wait_recv()
+        for step in range(n):
+            z_copy(k, step).wait_recv()
 
     def body(j, carry):
-        total = part_ref[mine, j].astype(jnp.float32)
+        total = part[mine, j].astype(jnp.float32)
         for k in range(1, fs):
             total = total + parts[k, j].astype(jnp.float32)
         summed[j] = total.astype(jnp.bfloat16)
@@ -233,42 +301,49 @@
         s_copy(k).start()
     own = pltpu.make_async_copy(summed.at[me], head_out.at[me], local)
     own.start()
+    grad.finish_far()
     for work in works:
-        work.forward()
+        work.arrive(n - 1)
     for work in works:
         work.finish()
     own.wait()
     for k in range(1, fs):
-        z_copy(k).wait_send()
+        for step in range(n):
+            z_copy(k, step).wait_send()
     for k in range(1, count):
         s_copy(k).wait()
 
 
-def middle(count, fs, key_rows, value_rows, part):
-    slots = part.shape[1:]
+def first(count, fs, out_grad, weight, key_rows, value_rows):
+    n = count // 2
+    low = jnp.bfloat16
+    slots = (count, weight.shape[0] // fs, out_grad.shape[0])
     return pl.pallas_call(
-        functools.partial(middle_kernel, count, fs),
+        functools.partial(first_kernel, count, fs),
         out_shape=[
-            jax.ShapeDtypeStruct((count,) + key_rows.shape, jnp.bfloat16),
-            jax.ShapeDtypeStruct((count,) + key_rows.shape, jnp.bfloat16),
-            jax.ShapeDtypeStruct(slots, jnp.bfloat16),
+            jax.ShapeDtypeStruct((count,) + out_grad.shape, low),
+            jax.ShapeDtypeStruct((count,) + key_rows.shape, low),
+            jax.ShapeDtypeStruct((count,) + key_rows.shape, low),
+            jax.ShapeDtypeStruct(slots, low),
         ],
-        in_specs=[ANY, ANY, VMEM],
-        out_specs=[ANY, ANY, ANY],
-        scratch_shapes=gather_sems(count // 2)
-        + gather_sems(count // 2)
+        in_specs=[ANY, VMEM, ANY, ANY],
+        out_specs=[VMEM, ANY, ANY, ANY],
+        scratch_shapes=gather_sems(n)
+        + gather_sems(n)
+        + gather_sems(n)
         + [
-            pltpu.VMEM((fs,) + slots, jnp.bfloat16),
-            pltpu.VMEM(slots, jnp.bfloat16),
-            DMA((fs,)),
-            DMA((fs,)),
+            pltpu.VMEM((fs,) + slots, low),
+            pltpu.VMEM((fs,) + slots, low),
+            pltpu.VMEM(slots, low),
+            DMA((fs * n,)),
+            DMA((fs * n,)),
             DMA((count,)),
             DMA((count,)),
             DMA,
         ],
-        compiler_params=params(2),
-        name="gather_keys_values_sum_head_grad",
-    )(key_rows, value_rows, part)
+        compiler_params=params(1),
+        name="gather_inputs_sum_head_grad",
+    )(out_grad, weight, key_rows, value_rows)
 
 
 def attend_kernel(blocks, pat, q_ref, k_ref, v_ref, g_ref, att_ref, qg_ref, kg_ref, vg_ref, *scratch):
@@ -375,7 +450,7 @@
         s_copy(k).wait_recv()
     for k in range(1, fs):
         z_copy(k).start()
-    for k in list(range(1, count // 2)) + [0]:
+    for k in works[0].order:
         for work in works:
             work.exchange(k)
     for work in works:
@@ -405,26 +480,55 @@
     )(key_sums, value_sums, att)
 
 
-def scatter_kernel(count, x, out, *scratch):
+def last_kernel(count, att_ref, w_ref, grad_ref, out, weight_out, partial, *scratch):
     greet(False, count, 0)
-    work = Scatter(count, x, out, *scratch)
-    work.start()
-    for k in list(range(1, count // 2)) + [0]:
-        work.exchange(k)
+    work = Scatter(count, partial, out, *scratch)
+    rows = out.shape[0]
+
+    def multiply(slot):
+        cols = pl.ds(pl.multiple_of(slot * rows, rows), rows)
+        partial[slot] = lax.dot_general(
+            att_ref[:, cols],
+            w_ref[...],
+            (((0,), (0,)), ((), ())),
+            preferred_element_type=jnp.float32,
+        ).astype(jnp.bfloat16)
+
+    for k in work.order:
+        multiply(work.near_slot(k))
+        work.near(k).start()
+    for k in work.order:
+        multiply(work.own_slot(k))
+        if k:
+            work.exchange(k)
+
+    def columns(i, carry):
+        cols = pl.ds(pl.multiple_of(i * 256, 256), 256)
+        weight_out[:, cols] = jnp.dot(
+            att_ref[...], grad_ref[:, cols], preferred_element_type=jnp.float32
+        )
+        return carry
+
+    lax.fori_loop(0, w_ref.shape[1] // 256, columns, 0)
+    work.exchange(0)
     work.finish()
 
 
-def scatter_projected(count, partial):
-    shape = partial.shape[1:]
+def last(count, att_all, weight, grad_all):
+    rows = grad_all.shape[0] // count
+    shape = (rows, grad_all.shape[1])
     return pl.pallas_call(
-        functools.partial(scatter_kernel, count),
-        out_shape=jax.ShapeDtypeStruct(shape, jnp.bfloat16),
-        in_specs=[VMEM],
-        out_specs=VMEM,
-        scratch_shapes=scatter_scratch(count, shape),
+        functools.partial(last_kernel, count),
+        out_shape=[
+            jax.ShapeDtypeStruct(shape, jnp.bfloat16),
+            jax.ShapeDtypeStruct(weight.shape, jnp.float32),
+        ],
+        in_specs=[VMEM, VMEM, VMEM],
+        out_specs=[VMEM, VMEM],
+        scratch_shapes=[pltpu.VMEM((count,) + shape, jnp.bfloat16)] + scatter_scratch(count, shape),
         compiler_params=params(4, 56),
-        name="sum_projected",
-    )(partial)
+        name="project_sum_weight_grad",
+    )(att_all, weight, grad_all)
 
 
 def shards(count, fs, queries, key_rows, value_rows, pattern, out_weight, out_grad):
@@ -432,18 +536,10 @@
     heads = width // HD
     part_e, heads_all, cols = out_weight.shape
     tokens = rows * count
-    f32, low = jnp.float32, jnp.bfloat16
-    weight = out_weight.reshape(part_e * heads_all, cols)
-
-    grad_all = gather_grad(count, out_grad).reshape(tokens, cols)
-    head_part = lax.dot_general(
-        weight, grad_all, (((1,), (1,)), ((), ())), preferred_element_type=f32
-    ).astype(low)
-    head_part = head_part.reshape(part_e, fs, heads, count, rows)
-    head_part = head_part.transpose(1, 3, 0, 2, 4).reshape(fs, count, part_e * heads, rows)
-
-    keys, values, head_grad = middle(count, fs, key_rows, value_rows, head_part)
-    grad_t = head_grad.reshape(count, part_e, heads, rows).transpose(2, 0, 1, 3)
+    weight = out_weight.transpose(1, 0, 2).reshape(heads_all * part_e, cols)
+
+    grad_all, keys, values, head_grad = first(count, fs, out_grad, weight, key_rows, value_rows)
+    grad_t = head_grad.reshape(count, heads, part_e, rows).transpose(1, 0, 2, 3)
     att_t, query_grad, key_sums, value_sums = attend(
         pattern,
         queries,
@@ -451,23 +547,17 @@
         values.reshape(tokens, width),
         grad_t.reshape(width, rows),
     )
-    att = att_t.reshape(heads, count, part_e, rows).transpose(1, 2, 0, 3)
+    att = att_t.reshape(heads, count, part_e, rows).transpose(1, 0, 2, 3)
     key_grad, value_grad, att_all = late(
         count,
         fs,
         key_sums.reshape(count, rows, width),
         value_sums.reshape(count, rows, width),
-        att.reshape(count, part_e * heads, rows),
+        att.reshape(count, heads * part_e, rows),
     )
-    att_all = att_all.reshape(fs, count, part_e, heads, rows).transpose(2, 0, 3, 1, 4)
-    att_all = att_all.reshape(part_e * heads_all, tokens)
-    partial = lax.dot_general(
-        att_all, weight, (((0,), (0,)), ((), ())), preferred_element_type=f32
-    ).astype(low)
-    projected = scatter_projected(count, partial.reshape(count, rows, cols))
-    weight_grad = lax.dot_general(
-        att_all, grad_all, (((1,), (0,)), ((), ())), preferred_element_type=f32
-    ).reshape(part_e, heads_all, cols)
+    att_all = att_all.transpose(0, 2, 1, 3).reshape(heads_all * part_e, tokens)
+    projected, weight_grad = last(count, att_all, weight, grad_all.reshape(tokens, cols))
+    weight_grad = weight_grad.reshape(heads_all, part_e, cols).transpose(1, 0, 2)
     return (projected, query_grad, key_grad, value_grad, weight_grad)
 
 

time: 233 us -> 187 us (0.80); the launches traced: 230 us -> 187 us
  Pallas kernels: 195 us -> 171 us
  matrix products: 15.4 us -> 0 us
  local copies, waits for them, and re-layouts: 18.6 us -> 15.1 us
    pallas_call x3 -> x2, Pallas kernels: 129 us -> 106 us  [the longest x1 68 us: first(): pl.pallas_call(functools.partial(first_kernel, count, fs), out_shape=[jax...]
    dot_general x3 -> x0, matrix products: 15.4 us -> none  [the longest x1 7.39 us: shards(): lax.dot_general(att_all, grad_all, (((1,), (0,)), ((), ())), preferred_el...]
    unnamed x29 -> x24, local copies, waits for them, and re-layouts: 12.2 us -> 5.71 us
    reshape x4 -> x3, local copies, waits for them, and re-layouts: 1.44 us -> 5.34 us  [the longest x1 4.53 us: shards(): weight_grad.reshape(heads_all, part_e, cols).transpose(1, 0, 2)]
    transpose x2, local copies, waits for them, and re-layouts: 0.27 us -> 4.03 us  [the longest x1 2.3 us: shards(): att_all = att_all.transpose(0, 2, 1, 3).reshape(heads_all * part_e, tokens)]
    pallas_call x2 -> x0, local copies, waits for them, and re-layouts: 2.52 us -> none  [the longest x1 2.3 us: late(): pl.pallas_call(functools.partial(late_kernel, count, fs), out_shape=[jax....]
where the time goes in v2:
time: 187 us
  Pallas kernels  171 us (91%)
  local copies, waits for them, and re-layouts  15.1 us (8%)
    pallas_call x1, Pallas kernels, first(): pl.pallas_call(functools.partial(first_kernel, count, fs), out_shape=[jax...  68 us
    pallas_call x1, Pallas kernels, late(): pl.pallas_call(functools.partial(late_kernel, count, fs), out_shape=[jax....  47.3 us
    pallas_call x1, Pallas kernels, last(): pl.pallas_call(functools.partial(last_kernel, count), out_shape=[jax.Shap...  38.3 us
    pallas_call x1, Pallas kernels, attend(): pl.pallas_call(functools.partial(attend_kernel, rows // BLK), grid_spec=p...  17.2 us
    unnamed x24, local copies, waits for them, and re-layouts  5.71 us
    reshape x1, local copies, waits for them, and re-layouts, shards(): weight_grad.reshape(heads_all, part_e, cols).transpose(1, 0, 2)  4.53 us

profile of v2, /device:TPU:9, one launch (start us, length us, event | category | flops | bytes accessed | tf_op | source)
XLA Modules:
  0.0 186.6 jit_solution(10577098058781527655)
XLA Ops:
  0.6 0.0 copy-start.2
  0.6 0.0 copy-start.4
  0.7 0.0 copy-start.3
  0.7 1.7 copy.11
  2.4 0.0 copy-start
  2.4 0.0 copy-start.5
  2.4 0.0 copy-start.6
  2.4 0.0 copy-done.2
  2.4 0.0 copy-done.4
  2.5 0.0 copy-done.3
  2.5 68.0 %gather_inputs_sum_head_grad.1 = (bf16[8,256,1536]{2,1,0:T(8,128)(2,1)}, bf16[8,256,768]{2,1,0:T(8,128)(2,1)}, bf16[8,256,768]{2,1,0:T(8,128)(2,1)}, bf16[8,96,256]{2,1,0:T(8,128)(2,1)S(1)}) custom-call(bf16[256,1536]{1,0:T(8,128)(2,1)S(1)} %copy-done.2, bf16[384,1536]{1,0:T(8,128)(2,1)S(1)} %bitcast.23, bf16[256,768]{1,0:T(8,128)(2,1)S(1)} %copy-done.3, ...), custom_call_target="tpu_custom_call" | custom-call | tf_op jit(solution)/shard_map/gather_inputs_sum_head_grad/pallas_call | solution.py:321
  70.5 0.0 copy-done.5
  70.5 0.0 copy-done.6
  70.5 17.2 %attend.1 = (bf16[768,256]{1,0:T(8,128)(2,1)S(1)}, bf16[256,768]{1,0:T(8,128)(2,1)}, bf16[2048,768]{1,0:T(8,128)(2,1)S(1)}, bf16[2048,768]{1,0:T(8,128)(2,1)}) custom-call(s32[2,8]{1,0:T(2,128)S(1)} %copy-done.6, bf16[256,768]{1,0:T(8,128)(2,1)S(1)} %copy-done.5, bf16[2048,768]{1,0:T(8,128)(2,1)} %bitcast.33, bf16[2048,768]{1,0:T(8,128)(2,1)} %bitcast.34, ...), custom_call_target="tpu_custom_call" | custom-call | tf_op jit(solution)/shard_map/attend/pallas_call | solution.py:396
  87.7 0.0 copy-done
  87.7 0.0 copy-start.1
  87.7 1.7 copy-done.1
  89.4 0.8 copy.13
  90.2 47.3 %sum_key_value_grads_gather_attended.1 = (bf16[256,768]{1,0:T(8,128)(2,1)}, bf16[256,768]{1,0:T(8,128)(2,1)}, bf16[4,8,96,256]{3,2,1,0:T(8,128)(2,1)}) custom-call(bf16[8,256,768]{2,1,0:T(8,128)(2,1)} %bitcast.25, bf16[8,256,768]{2,1,0:T(8,128)(2,1)} %bitcast.32, bf16[8,96,256]{2,1,0:T(8,128)(2,1)} %bitcast.38), custom_call_target="tpu_custom_call" | custom-call | tf_op jit(solution)/shard_map/sum_key_value_grads_gather_attended/pallas_call | solution.py:466
  137.4 2.3 %copy.14 = bf16[4,96,8,256]{3,2,1,0:T(8,128)(2,1)S(1)} copy(bf16[4,96,8,256]{3,1,2,0:T(8,128)(2,1)} %bitcast.37) | data formatting | bytes 3145728 | tf_op jit(solution)/shard_map/transpose | solution.py:558
  139.7 1.6 copy.16
  141.4 38.3 %project_sum_weight_grad.1 = (bf16[256,1536]{1,0:T(8,128)(2,1)}, f32[384,1536]{1,0:T(8,128)}) custom-call(bf16[384,2048]{1,0:T(8,128)(2,1)} %bitcast.31, bf16[384,1536]{1,0:T(8,128)(2,1)} %bitcast.24, bf16[2048,1536]{1,0:T(8,128)(2,1)} %bitcast.29), custom_call_target="tpu_custom_call" | custom-call | tf_op jit(solution)/shard_map/project_sum_weight_grad/pallas_call | solution.py:520
  179.7 0.0 copy-start.7
  179.7 0.0 copy-start.9
  179.7 4.5 %copy.18 = f32[24,16,1536]{2,0,1:T(8,128)} copy(f32[24,16,1536]{2,1,0:T(8,128)} %bitcast.36) | data formatting | bytes 4718592 | tf_op jit(solution)/shard_map/reshape | solution.py:560
  184.3 0.0 copy-start.8
  184.3 0.0 copy-done.7
  184.3 0.9 copy.22
  185.1 0.0 copy-done.9
  185.1 0.7 copy.23
  185.9 0.0 copy-done.8
  185.9 0.7 copy.24
  (1 shorter events, 0.0 us)
Async XLA Ops:
  0.6 1.8 copy-start.2
  0.6 1.8 copy-start.4
  0.7 1.8 copy-start.3
  2.4 85.3 %copy-start = (bf16[24,16,1536]{2,1,0:T(8,128)(2,1)}, bf16[24,16,1536]{2,1,0:T(8,128)(2,1)S(1)}, u32[]{:S(2)}) copy-start(bf16[24,16,1536]{2,1,0:T(8,128)(2,1)S(1)} %copy.11) | copy-start | bytes 3538948
  2.4 68.1 %copy-start.5 = (bf16[256,768]{1,0:T(8,128)(2,1)S(1)}, bf16[256,768]{1,0:T(8,128)(2,1)}, u32[]{:S(2)}) copy-start(bf16[256,768]{1,0:T(8,128)(2,1)} %q_ref.1) | copy-start | bytes 1179652
  2.4 68.1 %copy-start.6 = (s32[2,8]{1,0:T(2,128)S(1)}, s32[2,8]{1,0:T(2,128)}, u32[]{:S(2)}) copy-start(s32[2,8]{1,0:T(2,128)} %pat.1) | copy-start | bytes 196
  87.7 1.7 copy-start.1
  179.7 4.6 %copy-start.7 = (bf16[256,1536]{1,0:T(8,128)(2,1)S(1)}, bf16[256,1536]{1,0:T(8,128)(2,1)}, u32[]{:S(2)}) copy-start(bf16[256,1536]{1,0:T(8,128)(2,1)} %get-tuple-element.36) | copy-start | bytes 2359300
  179.7 5.4 %copy-start.9 = (bf16[256,768]{1,0:T(8,128)(2,1)S(1)}, bf16[256,768]{1,0:T(8,128)(2,1)}, u32[]{:S(2)}) copy-start(bf16[256,768]{1,0:T(8,128)(2,1)} %get-tuple-element.38) | copy-start | bytes 1179652
  184.3 1.6 copy-start.8

commit v3 on v2

--- a/solution.py
+++ b/solution.py
@@ -418,9 +418,49 @@
     )(pattern, queries, keys, values, grad_t)
 
 
+class Line:
+    def __init__(self, fs, out, up_send, up_recv, down_send, down_recv):
+        self.fs, self.out = fs, out
+        self.up_sems, self.down_sems = (up_send, up_recv), (down_send, down_recv)
+        self.mine = lax.axis_index("fsdp")
+
+    def copy(self, sems, shard, step, other):
+        slot = self.out.at[shard]
+        return remote(slot, slot, sems[0].at[step], sems[1].at[step], fsdp=other)
+
+    def sends(self, step, act):
+        mine, end = self.mine, self.fs - 1
+
+        @pl.when((mine >= step) & (mine < end))
+        def up():
+            act(self.copy(self.up_sems, mine - step, step, mine + 1))
+
+        @pl.when((mine + step <= end) & (mine > 0))
+        def down():
+            act(self.copy(self.down_sems, mine + step, step, mine - 1))
+
+    def start(self, step):
+        self.sends(step, lambda copy: copy.start())
+
+    def arrive(self, step):
+        mine, end = self.mine, self.fs - 1
+
+        @pl.when(mine - 1 >= step)
+        def below():
+            self.copy(self.up_sems, mine - 1 - step, step, mine - 1).wait_recv()
+
+        @pl.when(mine + 1 + step <= end)
+        def above():
+            self.copy(self.down_sems, mine + 1 + step, step, mine + 1).wait_recv()
+
+    def finish(self):
+        for step in range(self.fs - 1):
+            self.sends(step, lambda copy: copy.wait_send())
+
+
 def late_kernel(count, fs, kg_ref, vg_ref, att_ref, k_out, v_out, att_out, *scratch):
-    k_scratch, v_scratch = scratch[:7], scratch[7:14]
-    s_send, s_recv, z_send, z_recv, local = scratch[14:]
+    s_send, s_recv, local = scratch[14:17]
+    line = Line(fs, att_out, *scratch[17:])
     me = lax.axis_index("seq")
     mine = lax.axis_index("fsdp")
     greet(True, count, fs)
@@ -431,34 +471,36 @@
             att_ref.at[other], att_out.at[mine, me], s_send.at[k], s_recv.at[k], seq=other
         )
 
-    def z_copy(k):
-        other = lax.rem(mine + k, fs)
-        return remote(att_out.at[mine], att_out.at[mine], z_send.at[k], z_recv.at[k], fsdp=other)
-
     for k in range(1, count):
         s_copy(k).start()
     own = pltpu.make_async_copy(att_ref.at[me], att_out.at[mine, me], local)
     own.start()
     works = [
-        Scatter(count, kg_ref, k_out, *k_scratch),
-        Scatter(count, vg_ref, v_out, *v_scratch),
+        Scatter(count, kg_ref, k_out, *scratch[:7]),
+        Scatter(count, vg_ref, v_out, *scratch[7:14]),
     ]
     for work in works:
         work.start()
+    order = works[0].order
+    for work in works:
+        work.exchange(order[0])
     own.wait()
     for k in range(1, count):
         s_copy(k).wait_recv()
-    for k in range(1, fs):
-        z_copy(k).start()
-    for k in works[0].order:
-        for work in works:
-            work.exchange(k)
+    line.start(0)
+    for i in range(1, max(len(order), fs)):
+        if i < len(order):
+            for work in works:
+                work.exchange(order[i])
+        if i < fs:
+            line.arrive(i - 1)
+            if i < fs - 1:
+                line.start(i)
     for work in works:
         work.finish()
     for k in range(1, count):
         s_copy(k).wait_send()
-    for k in range(1, fs):
-        z_copy(k).wait()
+    line.finish()
 
 
 def late(count, fs, key_sums, value_sums, att):
@@ -474,25 +516,29 @@
         out_specs=[VMEM, VMEM, ANY],
         scratch_shapes=scatter_scratch(count, shape)
         + scatter_scratch(count, shape)
-        + [DMA((count,)), DMA((count,)), DMA((fs,)), DMA((fs,)), DMA],
+        + [DMA((count,)), DMA((count,)), DMA]
+        + [DMA((fs,)) for unused in range(4)],
         compiler_params=params(3, 56),
         name="sum_key_value_grads_gather_attended",
     )(key_sums, value_sums, att)
 
 
-def last_kernel(count, att_ref, w_ref, grad_ref, out, weight_out, partial, *scratch):
+def last_kernel(count, fs, part_e, att_ref, w_ref, grad_ref, out, weight_out, partial, flat, *scratch):
     greet(False, count, 0)
     work = Scatter(count, partial, out, *scratch)
     rows = out.shape[0]
 
     def multiply(slot):
-        cols = pl.ds(pl.multiple_of(slot * rows, rows), rows)
-        partial[slot] = lax.dot_general(
-            att_ref[:, cols],
-            w_ref[...],
-            (((0,), (0,)), ((), ())),
-            preferred_element_type=jnp.float32,
-        ).astype(jnp.bfloat16)
+        total = None
+        for f in range(fs):
+            term = lax.dot_general(
+                att_ref[f, slot],
+                w_ref[f],
+                (((0,), (0,)), ((), ())),
+                preferred_element_type=jnp.float32,
+            )
+            total = term if total is None else total + term
+        partial[slot] = total.astype(jnp.bfloat16)
 
     for k in work.order:
         multiply(work.near_slot(k))
@@ -502,33 +548,57 @@
         if k:
             work.exchange(k)
 
+    def flatten(j, carry):
+        at = pl.ds(pl.multiple_of(j * rows, rows), rows)
+        for f in range(fs):
+            flat[f, :, at] = att_ref[f, j]
+        return carry
+
+    lax.fori_loop(0, count, flatten, 0)
+
     def columns(i, carry):
         cols = pl.ds(pl.multiple_of(i * 256, 256), 256)
-        weight_out[:, cols] = jnp.dot(
-            att_ref[...], grad_ref[:, cols], preferred_element_type=jnp.float32
-        )
+        for f in range(fs):
+            product = jnp.dot(flat[f], grad_ref[:, cols], preferred_element_type=jnp.float32)
+            if part_e % 8:
+                weight_out[f, :, cols] = product
+                continue
+            heads = product.shape[0] // part_e
+            for h in range(heads):
+                weight_out[:, f * heads + h, cols] = product[h * part_e : (h + 1) * part_e]
         return carry
 
-    lax.fori_loop(0, w_ref.shape[1] // 256, columns, 0)
+    lax.fori_loop(0, w_ref.shape[2] // 256, columns, 0)
     work.exchange(0)
     work.finish()
 
 
-def last(count, att_all, weight, grad_all):
-    rows = grad_all.shape[0] // count
-    shape = (rows, grad_all.shape[1])
-    return pl.pallas_call(
-        functools.partial(last_kernel, count),
+def last(count, part_e, att_all, weight, grad_all):
+    fs, rows_here, cols = weight.shape
+    tokens = grad_all.shape[0]
+    shape = (tokens // count, cols)
+    heads_all = fs * rows_here // part_e
+    by_position = part_e % 8 == 0
+    grad_shape = (part_e, heads_all, cols) if by_position else weight.shape
+    projected, weight_grad = pl.pallas_call(
+        functools.partial(last_kernel, count, fs, part_e),
         out_shape=[
             jax.ShapeDtypeStruct(shape, jnp.bfloat16),
-            jax.ShapeDtypeStruct(weight.shape, jnp.float32),
+            jax.ShapeDtypeStruct(grad_shape, jnp.float32),
         ],
         in_specs=[VMEM, VMEM, VMEM],
         out_specs=[VMEM, VMEM],
-        scratch_shapes=[pltpu.VMEM((count,) + shape, jnp.bfloat16)] + scatter_scratch(count, shape),
+        scratch_shapes=[
+            pltpu.VMEM((count,) + shape, jnp.bfloat16),
+            pltpu.VMEM((fs, rows_here, tokens), jnp.bfloat16),
+        ]
+        + scatter_scratch(count, shape),
         compiler_params=params(4, 56),
         name="project_sum_weight_grad",
     )(att_all, weight, grad_all)
+    if not by_position:
+        weight_grad = weight_grad.reshape(heads_all, part_e, cols).transpose(1, 0, 2)
+    return projected, weight_grad
 
 
 def shards(count, fs, queries, key_rows, value_rows, pattern, out_weight, out_grad):
@@ -555,9 +625,13 @@
         value_sums.reshape(count, rows, width),
         att.reshape(count, heads * part_e, rows),
     )
-    att_all = att_all.transpose(0, 2, 1, 3).reshape(heads_all * part_e, tokens)
-    projected, weight_grad = last(count, att_all, weight, grad_all.reshape(tokens, cols))
-    weight_grad = weight_grad.reshape(heads_all, part_e, cols).transpose(1, 0, 2)
+    projected, weight_grad = last(
+        count,
+        part_e,
+        att_all,
+        weight.reshape(fs, heads * part_e, cols),
+        grad_all.reshape(tokens, cols),
+    )
     return (projected, query_grad, key_grad, value_grad, weight_grad)
 
 

time: 187 us -> 184 us (0.984); the launches traced: 187 us -> 181 us
  Pallas kernels: 171 us -> 167 us
  local copies, waits for them, and re-layouts: 15.1 us -> 12.8 us
    pallas_call x1, Pallas kernels: 47.3 us -> 41 us  [late(): pl.pallas_call(functools.partial(late_kernel, count, fs), out_shape=[jax....]
    unnamed x24, local copies, waits for them, and re-layouts: 5.71 us -> 10.3 us
    reshape x1 -> x0, local copies, waits for them, and re-layouts: 4.53 us -> none  [shards(): weight_grad.reshape(heads_all, part_e, cols).transpose(1, 0, 2)]
    pallas_call x1, Pallas kernels: 38.3 us -> 42.1 us  [last(): pl.pallas_call(functools.partial(last_kernel, count, fs, part_e), out_sha...]
    transpose x1 -> x0, local copies, waits for them, and re-layouts: 2.3 us -> none  [shards(): att_all = att_all.transpose(0, 2, 1, 3).reshape(heads_all * part_e, tokens)]
where the time goes in v3:
time: 184 us; the launch traced here: 181 us
  Pallas kernels  167 us (91%)
  local copies, waits for them, and re-layouts  12.8 us (7%)
    pallas_call x1, Pallas kernels, first(): pl.pallas_call(functools.partial(first_kernel, count, fs), out_shape=[jax...  66.9 us
    pallas_call x1, Pallas kernels, last(): pl.pallas_call(functools.partial(last_kernel, count, fs, part_e), out_sha...  42.1 us
    pallas_call x1, Pallas kernels, late(): pl.pallas_call(functools.partial(late_kernel, count, fs), out_shape=[jax....  41 us
    pallas_call x1, Pallas kernels, attend(): pl.pallas_call(functools.partial(attend_kernel, rows // BLK), grid_spec=p...  17.2 us
    unnamed x24, local copies, waits for them, and re-layouts  10.3 us

profile of v3, /device:TPU:9, one launch (start us, length us, event | category | flops | bytes accessed | tf_op | source)
XLA Modules:
  0.0 180.8 jit_solution(14580755913199271303)
XLA Ops:
  0.6 0.0 copy-start.6
  0.6 0.0 copy-start.5
  0.7 1.7 copy.11
  2.3 0.0 copy-start
  2.3 0.0 copy-start.2
  2.4 1.6 copy-done.2
  3.9 0.0 copy-start.3
  3.9 1.0 copy-done.3
  4.9 0.0 copy-start.4
  4.9 1.0 copy-done.4
  5.9 66.9 %gather_inputs_sum_head_grad.1 = (bf16[8,256,1536]{2,1,0:T(8,128)(2,1)}, bf16[8,256,768]{2,1,0:T(8,128)(2,1)}, bf16[8,256,768]{2,1,0:T(8,128)(2,1)}, bf16[8,96,256]{2,1,0:T(8,128)(2,1)S(1)}) custom-call(bf16[256,1536]{1,0:T(8,128)(2,1)S(1)} %copy-done.2, bf16[384,1536]{1,0:T(8,128)(2,1)S(1)} %bitcast.16, bf16[256,768]{1,0:T(8,128)(2,1)S(1)} %copy-done.3, ...), custom_call_target="tpu_custom_call" | custom-call | tf_op jit(solution)/shard_map/gather_inputs_sum_head_grad/pallas_call | solution.py:321
  72.8 0.0 copy-done.6
  72.8 0.0 copy-done.5
  72.8 17.2 %attend.1 = (bf16[768,256]{1,0:T(8,128)(2,1)S(1)}, bf16[256,768]{1,0:T(8,128)(2,1)}, bf16[2048,768]{1,0:T(8,128)(2,1)S(1)}, bf16[2048,768]{1,0:T(8,128)(2,1)}) custom-call(s32[2,8]{1,0:T(2,128)S(1)} %copy-done.6, bf16[256,768]{1,0:T(8,128)(2,1)S(1)} %copy-done.5, bf16[2048,768]{1,0:T(8,128)(2,1)} %bitcast.24, bf16[2048,768]{1,0:T(8,128)(2,1)} %bitcast.25, ...), custom_call_target="tpu_custom_call" | custom-call | tf_op jit(solution)/shard_map/attend/pallas_call | solution.py:396
  90.0 0.0 copy-done
  90.0 0.0 copy-start.1
  90.0 1.7 copy-done.1
  91.7 0.8 copy.13
  92.5 41.0 %sum_key_value_grads_gather_attended.1 = (bf16[256,768]{1,0:T(8,128)(2,1)}, bf16[256,768]{1,0:T(8,128)(2,1)}, bf16[4,8,96,256]{3,2,1,0:T(8,128)(2,1)}) custom-call(bf16[8,256,768]{2,1,0:T(8,128)(2,1)} %bitcast.18, bf16[8,256,768]{2,1,0:T(8,128)(2,1)} %bitcast.23, bf16[8,96,256]{2,1,0:T(8,128)(2,1)} %bitcast.26), custom_call_target="tpu_custom_call" | custom-call | tf_op jit(solution)/shard_map/sum_key_value_grads_gather_attended/pallas_call | solution.py:508
  133.5 0.0 copy-start.9
  133.5 0.0 copy-start.8
  133.5 42.1 %project_sum_weight_grad.1 = (bf16[256,1536]{1,0:T(8,128)(2,1)}, f32[16,24,1536]{2,1,0:T(8,128)}) custom-call(bf16[4,8,96,256]{3,2,1,0:T(8,128)(2,1)} %get-tuple-element.24.att_ref, bf16[4,96,1536]{2,1,0:T(8,128)(2,1)} %bitcast.17, bf16[2048,1536]{1,0:T(8,128)(2,1)} %bitcast.22), custom_call_target="tpu_custom_call" | custom-call | tf_op jit(solution)/shard_map/project_sum_weight_grad/pallas_call | solution.py:583
  175.6 0.0 copy-start.7
  175.6 2.2 %copy.19 = bf16[256,1536]{1,0:T(8,128)(2,1)} copy(bf16[256,1536]{1,0:T(8,128)(2,1)} %get-tuple-element.36) | data formatting | bytes 1572864
  177.8 0.0 copy-done.9
  177.9 0.7 copy.20
  178.6 0.0 copy-done.8
  178.6 0.7 copy.21
  179.3 0.0 copy-done.7
  179.3 1.4 copy.22
  (1 shorter events, 0.0 us)
Async XLA Ops:
  0.6 72.2 %copy-start.6 = (s32[2,8]{1,0:T(2,128)S(1)}, s32[2,8]{1,0:T(2,128)}, u32[]{:S(2)}) copy-start(s32[2,8]{1,0:T(2,128)} %pat.1) | copy-start | bytes 196
  0.6 72.2 %copy-start.5 = (bf16[256,768]{1,0:T(8,128)(2,1)S(1)}, bf16[256,768]{1,0:T(8,128)(2,1)}, u32[]{:S(2)}) copy-start(bf16[256,768]{1,0:T(8,128)(2,1)} %q_ref.1) | copy-start | bytes 1179652
  2.3 87.7 %copy-start = (bf16[24,16,1536]{2,1,0:T(8,128)(2,1)}, bf16[24,16,1536]{2,1,0:T(8,128)(2,1)S(1)}, u32[]{:S(2)}) copy-start(bf16[24,16,1536]{2,1,0:T(8,128)(2,1)S(1)} %copy.11) | copy-start | bytes 3538948
  2.3 1.6 copy-start.2
  3.9 1.0 copy-start.3
  4.9 1.0 copy-start.4
  90.0 1.7 copy-start.1
  133.5 44.4 %copy-start.9 = (bf16[256,768]{1,0:T(8,128)(2,1)S(1)}, bf16[256,768]{1,0:T(8,128)(2,1)}, u32[]{:S(2)}) copy-start(bf16[256,768]{1,0:T(8,128)(2,1)} %get-tuple-element.38) | copy-start | bytes 1179652
  133.5 45.1 %copy-start.8 = (bf16[256,768]{1,0:T(8,128)(2,1)S(1)}, bf16[256,768]{1,0:T(8,128)(2,1)}, u32[]{:S(2)}) copy-start(bf16[256,768]{1,0:T(8,128)(2,1)} %get-tuple-element.39) | copy-start | bytes 1179652
  175.6 3.7 %copy-start.7 = (f32[16,24,1536]{2,1,0:T(8,128)S(1)}, f32[16,24,1536]{2,1,0:T(8,128)}, u32[]{:S(2)}) copy-start(f32[16,24,1536]{2,1,0:T(8,128)} %get-tuple-element.40) | copy-start | bytes 7077892

commit v4 on v3

--- a/solution.py
+++ b/solution.py
@@ -341,7 +341,7 @@
             DMA((count,)),
             DMA,
         ],
-        compiler_params=params(1),
+        compiler_params=params(1, 61),
         name="gather_inputs_sum_head_grad",
     )(out_grad, weight, key_rows, value_rows)
 
@@ -359,24 +359,26 @@
     def dot(a, b, dims):
         return lax.dot_general(a, b, dims, preferred_element_type=f32)
 
+    held = []
     for j in range(blocks):
         here = slice(j * BLK, (j + 1) * BLK)
         for s in range(NSEL):
             at = pl.ds(pl.multiple_of(pat[j, s] * BLK, BLK), BLK)
-            k_set[s * BLK : (s + 1) * BLK, :] = k_ref[at, :]
-            v_set[s * BLK : (s + 1) * BLK, :] = v_ref[at, :]
+            k_set[j, s * BLK : (s + 1) * BLK, :] = k_ref[at, :]
+            v_set[j, s * BLK : (s + 1) * BLK, :] = v_ref[at, :]
+        held.append((here, dot(k_set[j], q_ref[here, :], nt) * scale))
+    for j, (here, scores) in enumerate(held):
         q = q_ref[here, :]
         g = g_ref[:, here]
-        scores = dot(k_set[...], q, nt) * scale
+        prob_grad = dot(v_set[j], g, nn)
         top = jnp.max(scores, axis=0, keepdims=True)
         exps = jnp.exp(scores - top)
         probs = exps * (1.0 / jnp.sum(exps, axis=0, keepdims=True))
         probs_low = probs.astype(low)
-        att_ref[:, here] = dot(v_set[...], probs_low, tn).astype(low)
-        prob_grad = dot(v_set[...], g, nn)
+        att_ref[:, here] = dot(v_set[j], probs_low, tn).astype(low)
         center = jnp.sum(probs * prob_grad, axis=0, keepdims=True)
         score_grad = (probs * (prob_grad - center)).astype(low)
-        qg_ref[here, :] = (dot(score_grad, k_set[...], tn) * scale).astype(low)
+        qg_ref[here, :] = (dot(score_grad, k_set[j], tn) * scale).astype(low)
         k_term = (dot(score_grad, q, nn) * scale).astype(low)
         v_term = dot(probs_low, g, nt).astype(low)
         for s in range(NSEL):
@@ -401,8 +403,8 @@
             in_specs=[by_col(rows), by_col(tokens), by_col(tokens), by_row],
             out_specs=[by_row, by_col(rows), by_col(tokens), by_col(tokens)],
             scratch_shapes=[
-                pltpu.VMEM((NSEL * BLK, HD), low),
-                pltpu.VMEM((NSEL * BLK, HD), low),
+                pltpu.VMEM((rows // BLK, NSEL * BLK, HD), low),
+                pltpu.VMEM((rows // BLK, NSEL * BLK, HD), low),
                 pltpu.VMEM((tokens, HD), jnp.float32),
                 pltpu.VMEM((tokens, HD), jnp.float32),
             ],
@@ -527,10 +529,18 @@
     greet(False, count, 0)
     work = Scatter(count, partial, out, *scratch)
     rows = out.shape[0]
+    packed = att_ref.shape[2] % 16 == 0
 
     def multiply(slot):
         total = None
-        for f in range(fs):
+        if packed:
+            total = lax.dot_general(
+                att_ref[:, slot].reshape(fs * att_ref.shape[2], rows),
+                w_ref[...].reshape(fs * att_ref.shape[2], w_ref.shape[2]),
+                (((0,), (0,)), ((), ())),
+                preferred_element_type=jnp.float32,
+            )
+        for f in range(0 if packed else fs):
             term = lax.dot_general(
                 att_ref[f, slot],
                 w_ref[f],

time: 184 us -> 180 us (0.978)
  Pallas kernels: 167 us -> 164 us
    unnamed x24 -> x16, local copies, waits for them, and re-layouts: 10.3 us -> 6.79 us
    pallas_call x1, Pallas kernels: 42.1 us -> 39.5 us  [last(): pl.pallas_call(functools.partial(last_kernel, count, fs, part_e), out_sha...]
    pallas_call x1, Pallas kernels: 17.2 us -> 14.7 us  [attend(): pl.pallas_call(functools.partial(attend_kernel, rows // BLK), grid_spec=p...]
where the time goes in v4:
time: 180 us; the launch traced here: 176 us
  Pallas kernels  164 us (91%)
  local copies, waits for them, and re-layouts  11.3 us (6%)
    pallas_call x1, Pallas kernels, first(): pl.pallas_call(functools.partial(first_kernel, count, fs), out_shape=[jax...  68.6 us
    pallas_call x1, Pallas kernels, late(): pl.pallas_call(functools.partial(late_kernel, count, fs), out_shape=[jax....  41.6 us
    pallas_call x1, Pallas kernels, last(): pl.pallas_call(functools.partial(last_kernel, count, fs, part_e), out_sha...  39.5 us
    pallas_call x1, Pallas kernels, attend(): pl.pallas_call(functools.partial(attend_kernel, rows // BLK), grid_spec=p...  14.7 us
    unnamed x16, local copies, waits for them, and re-layouts  6.79 us

profile of v4, /device:TPU:9, one launch (start us, length us, event | category | flops | bytes accessed | tf_op | source)
XLA Modules:
  0.0 176.4 jit_solution(10421552503789539831)
XLA Ops:
  0.6 0.0 copy-start.2
  0.6 0.0 copy-start.1
  0.7 2.7 %copy.11 = bf16[24,16,1536]{2,1,0:T(8,128)(2,1)} copy(bf16[24,16,1536]{2,0,1:T(8,128)(2,1)} %bitcast.26) | data formatting | bytes 2359296 | tf_op jit(solution)/shard_map/transpose | solution.py:619
  3.3 68.6 %gather_inputs_sum_head_grad.1 = (bf16[8,256,1536]{2,1,0:T(8,128)(2,1)}, bf16[8,256,768]{2,1,0:T(8,128)(2,1)}, bf16[8,256,768]{2,1,0:T(8,128)(2,1)}, bf16[8,96,256]{2,1,0:T(8,128)(2,1)}) custom-call(bf16[256,1536]{1,0:T(8,128)(2,1)} %grad_ref.1, bf16[384,1536]{1,0:T(8,128)(2,1)} %bitcast.19, bf16[256,768]{1,0:T(8,128)(2,1)} %k_ref.1, bf16[256,768]{1,0:T(8,128)(2,1)} %v_ref.1), custom_call_target="tpu_custom_call" | custom-call | tf_op jit(solution)/shard_map/gather_inputs_sum_head_grad/pallas_call | solution.py:321
  72.0 1.0 copy.12
  73.0 0.0 copy-done.2
  73.0 0.0 copy-done.1
  73.0 14.7 %attend.1 = (bf16[768,256]{1,0:T(8,128)(2,1)S(1)}, bf16[256,768]{1,0:T(8,128)(2,1)}, bf16[2048,768]{1,0:T(8,128)(2,1)S(1)}, bf16[2048,768]{1,0:T(8,128)(2,1)}) custom-call(s32[2,8]{1,0:T(2,128)S(1)} %copy-done.2, bf16[256,768]{1,0:T(8,128)(2,1)S(1)} %copy-done.1, bf16[2048,768]{1,0:T(8,128)(2,1)} %bitcast.23, bf16[2048,768]{1,0:T(8,128)(2,1)} %bitcast.24, ...), custom_call_target="tpu_custom_call" | custom-call | tf_op jit(solution)/shard_map/attend/pallas_call | solution.py:398
  87.7 0.0 copy-start
  87.7 1.7 copy-done
  89.3 0.8 copy.13
  90.1 41.6 %sum_key_value_grads_gather_attended.1 = (bf16[256,768]{1,0:T(8,128)(2,1)}, bf16[256,768]{1,0:T(8,128)(2,1)}, bf16[4,8,96,256]{3,2,1,0:T(8,128)(2,1)}) custom-call(bf16[8,256,768]{2,1,0:T(8,128)(2,1)} %bitcast.16, bf16[8,256,768]{2,1,0:T(8,128)(2,1)} %bitcast.22, bf16[8,96,256]{2,1,0:T(8,128)(2,1)} %bitcast.25), custom_call_target="tpu_custom_call" | custom-call | tf_op jit(solution)/shard_map/sum_key_value_grads_gather_attended/pallas_call | solution.py:510
  131.7 0.0 copy-start.5
  131.7 0.0 copy-start.4
  131.7 39.5 %project_sum_weight_grad.1 = (bf16[256,1536]{1,0:T(8,128)(2,1)}, f32[16,24,1536]{2,1,0:T(8,128)}) custom-call(bf16[4,8,96,256]{3,2,1,0:T(8,128)(2,1)} %get-tuple-element.24.att_ref, bf16[4,96,1536]{2,1,0:T(8,128)(2,1)} %bitcast.20, bf16[2048,1536]{1,0:T(8,128)(2,1)} %bitcast.21), custom_call_target="tpu_custom_call" | custom-call | tf_op jit(solution)/shard_map/project_sum_weight_grad/pallas_call | solution.py:593
  171.3 0.0 copy-start.3
  171.3 2.2 %copy.19 = bf16[256,1536]{1,0:T(8,128)(2,1)} copy(bf16[256,1536]{1,0:T(8,128)(2,1)} %get-tuple-element.36) | data formatting | bytes 1572864
  173.5 0.0 copy-done.5
  173.5 0.7 copy.20
  174.3 0.0 copy-done.4
  174.3 0.7 copy.21
  175.0 0.0 copy-done.3
  175.0 1.4 copy.22
Async XLA Ops:
  0.6 72.4 %copy-start.2 = (s32[2,8]{1,0:T(2,128)S(1)}, s32[2,8]{1,0:T(2,128)}, u32[]{:S(2)}) copy-start(s32[2,8]{1,0:T(2,128)} %pat.1) | copy-start | bytes 196
  0.6 72.4 %copy-start.1 = (bf16[256,768]{1,0:T(8,128)(2,1)S(1)}, bf16[256,768]{1,0:T(8,128)(2,1)}, u32[]{:S(2)}) copy-start(bf16[256,768]{1,0:T(8,128)(2,1)} %q_ref.1) | copy-start | bytes 1179652
  87.7 1.7 copy-start
  131.7 41.8 %copy-start.5 = (bf16[256,768]{1,0:T(8,128)(2,1)S(1)}, bf16[256,768]{1,0:T(8,128)(2,1)}, u32[]{:S(2)}) copy-start(bf16[256,768]{1,0:T(8,128)(2,1)} %get-tuple-element.38) | copy-start | bytes 1179652
  131.7 42.5 %copy-start.4 = (bf16[256,768]{1,0:T(8,128)(2,1)S(1)}, bf16[256,768]{1,0:T(8,128)(2,1)}, u32[]{:S(2)}) copy-start(bf16[256,768]{1,0:T(8,128)(2,1)} %get-tuple-element.39) | copy-start | bytes 1179652
  171.3 3.7 %copy-start.3 = (f32[16,24,1536]{2,1,0:T(8,128)S(1)}, f32[16,24,1536]{2,1,0:T(8,128)}, u32[]{:S(2)}) copy-start(f32[16,24,1536]{2,1,0:T(8,128)} %get-tuple-element.40) | copy-start | bytes 7077892
